TPU v7x, 32 devices: a whole 2x2x4 slice. The times are simulated.
32 devices in a mesh: seq: 16 (over z, y, x), tp: 2 (over core).
Axes of the slice: x: 2, y: 2, z: 4, core: 2. Of those that a mesh axis runs over, the one named last changes fastest.
Arguments:
- query_rows: bfloat16 [8192, 1536], P('seq', 'tp'), may hold values from -48 to 48
- key_rows: bfloat16 [8192, 1536], P('seq', 'tp'), may hold values from -8 to 8
- value_rows: bfloat16 [8192, 1536], P('seq', 'tp'), may hold values from -6 to 6
- frame_counts: int32 [12], replicated, may hold values from 1 to 4, 32 in all
- out_weight: bfloat16 [1536, 3072], P('tp'), may hold values from -0.15625 to 0.15625
Outputs:
- mixed: bfloat16 [8192, 3072], P('seq', 'tp')
Inputs may be any that keep to these rules, and one draw needn't show every extreme that they name: `frame_counts`: the 12 clips' frame counts sum to 32; the longest has exactly 4 frames.
All inputs are finite; a program needn't handle non-finite values.
Results may differ from a plain program's by a relative error of at most 0.015.
Values may be sent and summed in bfloat16 or wider, within the bound.
A program may use at most 64 MiB of HBM per device.

v0:
```python
import math

import jax
import jax.numpy as jnp
from jax import lax
from jax.sharding import PartitionSpec as P

RT = 16
RH = 56
RW = 56
PH = 16
PW = 16
HEAD_DIM = 128


NEG_FILL = -1e30
ROPE_BASE = 256.0


def from_behind(value, axis, by):
    count = lax.axis_size(axis)
    return lax.ppermute(value, axis, [(i, (i + by) % count) for i in range(count)])


def clip_layout(frame_counts, token_index):
    clip_sizes = frame_counts * (PH * PW)
    clip_ends = jnp.cumsum(clip_sizes)
    passed = token_index[:, None] >= clip_ends[None, :]
    clip_id = jnp.sum(passed.astype(jnp.int32), axis=1)
    clip_start = jnp.sum(jnp.where(passed, clip_sizes[None, :], 0), axis=1)
    return (clip_id, token_index - clip_start)


def rotate(features, offset):
    frame_size = PH * PW
    coordinates = (offset // frame_size, offset % frame_size // PW, offset % PW)
    pieces = []
    section_start = 0
    for section_width, coordinate in zip((RT, RH, RW), coordinates):
        half_width = section_width // 2
        section = features[:, :, section_start : section_start + section_width]
        first_half = section[..., :half_width]
        second_half = section[..., half_width:]
        frequency = jnp.exp(
            -(2.0 * jnp.arange(half_width, dtype=jnp.float32) / section_width) * math.log(ROPE_BASE)
        )
        phase_angle = coordinate.astype(jnp.float32)[:, None] * frequency[None, :]
        cosine = jnp.cos(phase_angle)[:, None, :]
        sine_part = jnp.sin(phase_angle)[:, None, :]
        pieces.append(first_half * cosine - second_half * sine_part)
        pieces.append(second_half * cosine + first_half * sine_part)
        section_start = section_start + section_width
    return jnp.concatenate(pieces, axis=2)


def per_device(query_rows, key_rows, value_rows, frame_counts, out_weight):
    tok_count = query_rows.shape[0]
    head_count = query_rows.shape[1] // HEAD_DIM
    cycle_size = lax.axis_size("seq")
    position = lax.axis_index("seq")
    offsets = jnp.arange(tok_count, dtype=jnp.int32)
    local_index = position * tok_count + offsets
    query_clip, query_offset = clip_layout(frame_counts, local_index)
    rotated_q = rotate(
        query_rows.astype(jnp.float32).reshape(tok_count, head_count, HEAD_DIM), query_offset
    ).astype(jnp.bfloat16)
    rotated_k = rotate(
        key_rows.astype(jnp.float32).reshape(tok_count, head_count, HEAD_DIM), query_offset
    ).astype(jnp.bfloat16)
    rotated_k = rotated_k.reshape(tok_count, head_count * HEAD_DIM)
    scale_factor = HEAD_DIM ** (-0.5)
    frame_total = tok_count * cycle_size // (PH * PW)
    longest = frame_total // 8 * PH * PW
    reach_count = min((longest + tok_count - 1) // tok_count, cycle_size - 1)

    def absorb(state, key_block, value_block, key_index, key_valid):
        run_max, run_total, accum = state
        block_len = key_block.shape[0]
        key_heads = key_block.reshape(block_len, head_count, HEAD_DIM)
        value_heads = value_block.reshape(block_len, head_count, HEAD_DIM)
        key_clip, unused_offset = clip_layout(frame_counts, key_index)
        scores = (
            jnp.einsum("thd,shd->hts", rotated_q, key_heads, preferred_element_type=jnp.float32)
            * scale_factor
        )
        allowed = (query_clip[:, None] == key_clip[None, :]) & key_valid[None, :]
        scores = jnp.where(allowed[None], scores, NEG_FILL)
        new_max = jnp.maximum(run_max, jnp.max(scores, axis=2))
        expo = jnp.where(allowed[None], jnp.exp(scores - new_max[:, :, None]), 0.0)
        rescale = jnp.exp(run_max - new_max)
        run_total = run_total * rescale + jnp.sum(expo, axis=2)
        accum = accum * rescale[:, :, None] + jnp.einsum(
            "hts,shd->htd",
            expo.astype(jnp.bfloat16),
            value_heads,
            preferred_element_type=jnp.float32,
        )
        return (new_max, run_total, accum)

    start_state = (
        jnp.full((head_count, tok_count), NEG_FILL, jnp.float32),
        jnp.zeros((head_count, tok_count), jnp.float32),
        jnp.zeros((head_count, tok_count, HEAD_DIM), jnp.float32),
    )
    stacked = jnp.stack([rotated_k, value_rows])
    always_valid = jnp.ones((tok_count,), jnp.bool_)
    ahead = from_behind(stacked, "seq", -reach_count)
    ahead_source = (position + reach_count) % cycle_size
    first_state = absorb(
        start_state, ahead[0], ahead[1], ahead_source * tok_count + offsets, always_valid
    )

    def onward(distance, carry):
        pair, state = carry
        pair = from_behind(pair, "seq", 1)
        source = (position + reach_count - distance + cycle_size) % cycle_size
        state = absorb(state, pair[0], pair[1], source * tok_count + offsets, always_valid)
        return (pair, state)

    final_state = lax.fori_loop(1, 2 * reach_count + 1, onward, (ahead, first_state))[1]
    run_max, run_total, accum = final_state
    attended = (
        (accum / run_total[:, :, None])
        .transpose(1, 0, 2)
        .reshape(tok_count, head_count * HEAD_DIM)
        .astype(jnp.bfloat16)
    )
    head_terms = jnp.dot(attended, out_weight, preferred_element_type=jnp.float32)
    mixed = lax.psum_scatter(head_terms.astype(jnp.bfloat16), "tp", scatter_dimension=1, tiled=True)
    return mixed


def solution(mesh):
    return jax.shard_map(
        per_device,
        mesh=mesh,
        in_specs=(P("seq", "tp"), P("seq", "tp"), P("seq", "tp"), P(), P("tp", None)),
        out_specs=P("seq", "tp"),
        check_vma=False,
    )
```

profile of v0, /device:TPU:0, one launch (start us, length us, event | category | flops | bytes accessed | tf_op | source)
XLA Modules:
  0.0 310.2 jit_solution(15808066672719563749)
XLA Ops:
  7.6 1.4 copy.57
  13.1 1.8 copy.89
  14.9 1.7 copy.90
  16.5 1.7 copy.95
  18.2 1.7 copy.96
  20.9 2.7 copy.93
  23.6 1.7 copy.94
  27.1 2.5 copy.85
  29.7 1.6 copy.86
  31.3 2.5 copy.91
  33.9 1.7 copy.92
  35.5 1.9 multiply_cosine_fusion
  37.4 5.4 %add_convert_fusion = (bf16[512,6,28]{2,0,1:T(8,128)(2,1)}, bf16[512,6,28]{2,0,1:T(8,128)(2,1)}, bf16[512,6,28]{2,0,1:T(8,128)(2,1)}, bf16[512,6,28]{2,0,1:T(8,128)(2,1)}) fusion(f32[512,6,28]{2,0,1:T(8,128)} %copy.95, f32[512,6,28]{2,0,1:T(8,128)} %copy.96, f32[512,28]{1,0:T(8,128)S(1)} %get-tuple-element.335, f32[512,28]{1,0:T(8,128)S(1)} %get-tuple-element.334, ...), kind=kLoop, calls=%fused_computation.28 | loop fusion | flops 1376256 | bytes 2179072 | tf_op jit(solution)/shard_map/convert.7
  42.9 2.3 add_convert_fusion.1
  46.8 2.3 add_convert_fusion.2
  49.8 5.2 %concatenate.8 = bf16[512,6,128]{2,0,1:T(8,128)(2,1)} concatenate(bf16[512,6,8]{2,0,1:T(8,128)(2,1)} %get-tuple-element.330, bf16[512,6,8]{2,0,1:T(8,128)(2,1)} %get-tuple-element.331, bf16[512,6,28]{2,0,1:T(8,128)(2,1)S(1)} %copy-done.9, bf16[512,6,28]{2,0,1:T(8,128)(2,1)S(1)} %copy-done.10, bf16[512,6,28]{2,0,1:T(8,128)(2,1)S(1)} %copy-done.7, bf16[512,6,28]{2,0,1:T(8,128)(2,1)S(1)} %copy-done.8), dimensions={2} | concatenate | bytes 1572864 | tf_op jit(solution)/shard_map/concatenate | solution.py:53
  55.0 1.5 copy.66
  56.7 1.3 pad_maximum_fusion
  58.0 6.0 %collective-permute-start.1 = (bf16[2,512,768]{1,2,0:T(8,128)(2,1)}, bf16[2,512,768]{1,2,0:T(8,128)(2,1)}, u32[]{:S(2)}, u32[]{:S(2)}) collective-permute-start(bf16[2,512,768]{1,2,0:T(8,128)(2,1)} %pad_maximum_fusion), channel_id=1, source_target_pairs={{0,28},{2,30},{4,0},{6,2},{8,4},{10,6},{12,8},{14,10},{16,12},{18,... | collective-permute-start | bytes 4718600 | tf_op jit(solution)/shard_map/ppermute | solution.py:22
  64.0 4.7 %concatenate.9 = bf16[512,6,128]{2,0,1:T(8,128)(2,1)S(1)} concatenate(bf16[512,6,8]{2,0,1:T(8,128)(2,1)} %get-tuple-element.305, bf16[512,6,8]{2,0,1:T(8,128)(2,1)} %get-tuple-element.304, bf16[512,6,28]{2,0,1:T(8,128)(2,1)} %get-tuple-element.303, bf16[512,6,28]{2,0,1:T(8,128)(2,1)} %get-tuple-element.302, bf16[512,6,28]{2,0,1:T(8,128)(2,1)} %get-tuple-element.301, ...), dimensions={2} | concatenate | bytes 1572864 | tf_op jit(solution)/shard_map/concatenate | solution.py:53
  69.0 29.0 %collective-permute-done.1 = bf16[2,512,768]{1,2,0:T(8,128)(2,1)} collective-permute-done((bf16[2,512,768]{1,2,0:T(8,128)(2,1)}, bf16[2,512,768]{1,2,0:T(8,128)(2,1)}, u32[]{:S(2)}, u32[]{:S(2)}) %collective-permute-start.1) | collective-permute-done | bytes 1572896 | tf_op jit(solution)/shard_map/ppermute | solution.py:22
  98.0 1.5 fusion.38
  99.5 1.3 fusion.13
  100.8 1.5 fusion.15
  102.4 3.4 %fusion.19 = f32[6,512,128]{2,1,0:T(8,128)} fusion(bf16[512,6,128]{0,2,1:T(8,128)(2,1)S(1)} %bitcast.50, f32[6,512,512]{1,2,0:T(8,128)S(1)} %get-tuple-element.348, f32[6,512]{1,0:T(8,128)S(1)} %broadcast_maximum_fusion, pred[512,512]{0,1:T(8,128)(4,1)S(1)} %broadcast_compare_fusion.1, f32[6,512]{1,0:T(8,128)S(1)} %get-tuple-element.332), kind=kOutput, calls=%fused_computation.40 | convolution fusion | flops 410910720 | bytes 8937472 | tf_op jit(solution)/shard_map/hts,shd->htd/dot_general | solution.py:92
  105.8 182.1 %while.22 = (s32[]{:T(128)}, bf16[2,512,768]{1,2,0:T(8,128)(2,1)}, f32[6,512]{1,0:T(8,128)S(1)}, f32[6,512]{1,0:T(8,128)S(1)}, f32[6,512,128]{2,1,0:T(8,128)}, /...) while((s32[]{:T(128)}, bf16[2,512,768]{1,2,0:T(8,128)(2,1)}, ...), condition=%wide.region_11.12_spmd.clone, body=%wide.region_6.11_spmd.clone.sunk | while | flops 826826880 | bytes 50801260 | solution.py:120
  105.8 1.5 collective-permute-start
  107.8 37.8 %collective-permute-done = bf16[2,512,768]{1,2,0:T(8,128)(2,1)S(1)} collective-permute-done((bf16[2,512,768]{1,2,0:T(8,128)(2,1)}, bf16[2,512,768]{1,2,0:T(8,128)(2,1)S(1)}, u32[]{:S(2)}, u32[]{:S(2)}) %collective-permute-start) | collective-permute-done | bytes 1572896 | tf_op jit(solution)/shard_map/while/body/eval_jaxpr/ppermute | solution.py:22
  145.7 1.3 fusion.63
  147.1 1.5 fusion.64
  148.7 2.8 multiply_add_fusion.5
  151.4 1.2 copy.108
  153.6 37.9 %collective-permute-done = bf16[2,512,768]{1,2,0:T(8,128)(2,1)S(1)} collective-permute-done((bf16[2,512,768]{1,2,0:T(8,128)(2,1)}, bf16[2,512,768]{1,2,0:T(8,128)(2,1)S(1)}, u32[]{:S(2)}, u32[]{:S(2)}) %collective-permute-start) | collective-permute-done | bytes 1572896 | tf_op jit(solution)/shard_map/while/body/eval_jaxpr/ppermute | solution.py:22
  191.6 1.3 fusion.63
  193.0 1.5 fusion.64
  194.5 2.8 multiply_add_fusion.5
  199.5 37.0 %collective-permute-done = bf16[2,512,768]{1,2,0:T(8,128)(2,1)S(1)} collective-permute-done((bf16[2,512,768]{1,2,0:T(8,128)(2,1)}, bf16[2,512,768]{1,2,0:T(8,128)(2,1)S(1)}, u32[]{:S(2)}, u32[]{:S(2)}) %collective-permute-start) | collective-permute-done | bytes 1572896 | tf_op jit(solution)/shard_map/while/body/eval_jaxpr/ppermute | solution.py:22
  236.6 1.3 fusion.63
  237.9 1.5 fusion.64
  239.5 2.8 multiply_add_fusion.5
  244.4 36.0 %collective-permute-done = bf16[2,512,768]{1,2,0:T(8,128)(2,1)S(1)} collective-permute-done((bf16[2,512,768]{1,2,0:T(8,128)(2,1)}, bf16[2,512,768]{1,2,0:T(8,128)(2,1)S(1)}, u32[]{:S(2)}, u32[]{:S(2)}) %collective-permute-start) | collective-permute-done | bytes 1572896 | tf_op jit(solution)/shard_map/while/body/eval_jaxpr/ppermute | solution.py:22
  280.6 1.3 fusion.63
  281.9 1.5 fusion.64
  283.5 2.8 multiply_add_fusion.5
  286.3 1.2 copy.108
  287.9 1.9 copy.78
  290.0 6.4 %convolution_convert_fusion = bf16[512,3072]{1,0:T(8,128)(2,1)} fusion(bf16[512,768]{0,1:T(8,128)(2,1)S(1)} %bitcast.51, bf16[768,3072]{1,0:T(8,128)(2,1)} %param.11), kind=kOutput, calls=%fused_computation.21 | convolution fusion | flops 2417491968 | bytes 8650752 | tf_op jit(solution)/shard_map/dot_general | solution.py:128
  296.4 6.9 %reduce-scatter.2.cloned.1.call-done = bf16[512,1536]{1,0:T(8,128)(2,1)} async-done(((bf16[512,3072]{1,0:T(8,128)(2,1)}), bf16[512,1536]{1,0:T(8,128)(2,1)}) %reduce-scatter.2.cloned.1.call-update) | async-done | bytes 1572880 | tf_op jit(solution)/shard_map/reduce_scatter | solution.py:129
  (121 shorter events, 17.8 us)
Async XLA Ops:
  6.5 296.8 %reduce-scatter.2.cloned.1.call-start = ((), (), s32[]{:S(2)}) async-start(), calls=%async_computation.1 | async-start | bytes 4718592 | tf_op jit(solution)/shard_map/reduce_scatter | solution.py:129
  9.0 1.1 copy-start.15
  10.4 1.8 copy-start.20
  20.9 2.7 copy-start.13
  25.3 4.4 %copy-start.17 = (f32[512,6,8]{0,2,1:T(8,128)S(1)}, f32[512,6,8]{0,2,1:T(8,128)}, u32[]{:S(2)}) copy-start(f32[512,6,8]{0,2,1:T(8,128)} %get-tuple-element.325) | copy-start | bytes 294916
  31.3 2.5 copy-start.18
  31.3 4.2 %copy-start.19 = (f32[28]{0:T(128)S(1)}, f32[28]{0:T(128)}, u32[]{:S(2)}) copy-start(f32[28]{0:T(128)} %multiply_exponential_fusion) | copy-start | bytes 340
  37.4 5.4 %copy-start = (f32[512,6,28]{2,0,1:T(8,128)S(1)}, f32[512,6,28]{2,0,1:T(8,128)}, u32[]{:S(2)}) copy-start(f32[512,6,28]{2,0,1:T(8,128)} %copy.93) | copy-start | bytes 1032196
  37.4 5.4 %copy-start.1 = (f32[512,6,28]{2,0,1:T(8,128)S(1)}, f32[512,6,28]{2,0,1:T(8,128)}, u32[]{:S(2)}) copy-start(f32[512,6,28]{2,0,1:T(8,128)} %copy.94) | copy-start | bytes 1032196
  42.8 2.4 copy-start.2
  42.8 2.8 copy-start.3
  42.8 3.5 %copy-start.4 = (f32[512,6,8]{2,0,1:T(8,128)S(1)}, f32[512,6,8]{2,0,1:T(8,128)}, u32[]{:S(2)}) copy-start(f32[512,6,8]{2,0,1:T(8,128)} %copy.91) | copy-start | bytes 294916
  42.8 3.9 %copy-start.5 = (f32[512,6,8]{2,0,1:T(8,128)S(1)}, f32[512,6,8]{2,0,1:T(8,128)}, u32[]{:S(2)}) copy-start(f32[512,6,8]{2,0,1:T(8,128)} %copy.92) | copy-start | bytes 294916
  42.9 3.9 %copy-start.14 = (f32[512,8]{1,0:T(8,128)S(1)}, f32[512,8]{1,0:T(8,128)}, u32[]{:S(2)}) copy-start(f32[512,8]{1,0:T(8,128)} %copy.61) | copy-start | bytes 49156
  46.8 2.3 copy-start.7
  46.8 2.3 copy-start.8
  46.8 2.3 copy-start.9
  46.8 3.0 copy-start.10
  55.0 1.5 copy-start.16
  56.7 7.3 %copy-start.6 = (bf16[512,6,28]{2,0,1:T(8,128)(2,1)S(1)}, bf16[512,6,28]{2,0,1:T(8,128)(2,1)}, u32[]{:S(2)}) copy-start(bf16[512,6,28]{2,0,1:T(8,128)(2,1)} %get-tuple-element.300) | copy-start | bytes 516100
  58.0 40.0 %collective-permute-start.1 = (bf16[2,512,768]{1,2,0:T(8,128)(2,1)}, bf16[2,512,768]{1,2,0:T(8,128)(2,1)}, u32[]{:S(2)}, u32[]{:S(2)}) collective-permute-start(bf16[2,512,768]{1,2,0:T(8,128)(2,1)} %pad_maximum_fusion), channel_id=1, source_target_pairs={{0,28},{2,30},{4,0},{6,2},{8,4},{10,6},{12,8},{14,10},{16,12},{18,... | collective-permute-start | bytes 4718600 | tf_op jit(solution)/shard_map/ppermute | solution.py:22
  102.4 3.4 %copy-start.21 = (s32[12]{0:T(128)S(1)}, s32[12]{0:T(128)}, u32[]{:S(2)}) copy-start(s32[12]{0:T(128)} %param.10) | copy-start | bytes 148
  105.8 39.8 %collective-permute-start = (bf16[2,512,768]{1,2,0:T(8,128)(2,1)}, bf16[2,512,768]{1,2,0:T(8,128)(2,1)S(1)}, u32[]{:S(2)}, u32[]{:S(2)}) collective-permute-start(bf16[2,512,768]{1,2,0:T(8,128)(2,1)} %get-tuple-element.433), channel_id=1, source_target_pairs={{0,2},{2,4},{4,6},{6,8},{8,10},{10,12},{12,14},{14,16},{16,18},{18... | collective-permute-start | bytes 4718600 | tf_op jit(solution)/shard_map/while/body/eval_jaxpr/ppermute | solution.py:22
  147.1 1.6 copy-start.11
  151.4 1.7 copy-start.12
  153.1 38.4 %collective-permute-start = (bf16[2,512,768]{1,2,0:T(8,128)(2,1)}, bf16[2,512,768]{1,2,0:T(8,128)(2,1)S(1)}, u32[]{:S(2)}, u32[]{:S(2)}) collective-permute-start(bf16[2,512,768]{1,2,0:T(8,128)(2,1)} %get-tuple-element.433), channel_id=1, source_target_pairs={{0,2},{2,4},{4,6},{6,8},{8,10},{10,12},{12,14},{14,16},{16,18},{18... | collective-permute-start | bytes 4718600 | tf_op jit(solution)/shard_map/while/body/eval_jaxpr/ppermute | solution.py:22
  193.0 1.6 copy-start.11
  197.3 1.7 copy-start.12
  199.0 37.5 %collective-permute-start = (bf16[2,512,768]{1,2,0:T(8,128)(2,1)}, bf16[2,512,768]{1,2,0:T(8,128)(2,1)S(1)}, u32[]{:S(2)}, u32[]{:S(2)}) collective-permute-start(bf16[2,512,768]{1,2,0:T(8,128)(2,1)} %get-tuple-element.433), channel_id=1, source_target_pairs={{0,2},{2,4},{4,6},{6,8},{8,10},{10,12},{12,14},{14,16},{16,18},{18... | collective-permute-start | bytes 4718600 | tf_op jit(solution)/shard_map/while/body/eval_jaxpr/ppermute | solution.py:22
  237.9 1.6 copy-start.11
  242.3 1.7 copy-start.12
  243.9 36.6 %collective-permute-start = (bf16[2,512,768]{1,2,0:T(8,128)(2,1)}, bf16[2,512,768]{1,2,0:T(8,128)(2,1)S(1)}, u32[]{:S(2)}, u32[]{:S(2)}) collective-permute-start(bf16[2,512,768]{1,2,0:T(8,128)(2,1)} %get-tuple-element.433), channel_id=1, source_target_pairs={{0,2},{2,4},{4,6},{6,8},{8,10},{10,12},{12,14},{14,16},{16,18},{18... | collective-permute-start | bytes 4718600 | tf_op jit(solution)/shard_map/while/body/eval_jaxpr/ppermute | solution.py:22
  281.9 1.6 copy-start.11
  286.3 1.7 copy-start.12
Sparse Core Ops, SparseCore 0:
  296.5 6.7 reduce-scatter.1
where the time goes:
time: 311 us; the launch traced here: 310 us
  waiting for transfers between devices  185 us (59%)
  local copies, waits for them, and re-layouts  50.4 us (16%)
  matrix products  27.4 us (9%)
  other arithmetic  26.1 us (8%)
  between operations  13.7 us (4%)
  starting transfers between devices  7.51 us (2%)
    ppermute x5, waiting for transfers between devices, from_behind(): lax.ppermute(value, axis, [(i, (i + by) % count) for i in range(count)])  178 us
    unnamed x55, local copies, waits for them, and re-layouts  25 us
    dot_general x5, matrix products, absorb(): jnp.einsum('hts,shd->htd', expo.astype(jnp.bfloat16), value_heads, prefer...  14.5 us
    concatenate x3, local copies, waits for them, and re-layouts, rotate(): return jnp.concatenate(pieces, axis=2)  11.3 us
    another operation x8, other arithmetic  10.9 us
    reduce_sum x5, other arithmetic, absorb(): run_total = run_total * rescale + jnp.sum(expo, axis=2)  7.57 us
    ppermute x5, starting transfers between devices, from_behind(): lax.ppermute(value, axis, [(i, (i + by) % count) for i in range(count)])  7.5 us
    reduce_scatter x1, waiting for transfers between devices, per_device(): lax.psum_scatter(head_terms.astype(jnp.bfloat16), 'tp', scatter_dimension...  6.94 us
  transfers between devices with their start and end apart: 6, of which 6 were waited for; matrix products, arithmetic and copies ran while one was open for 2% of the time, Pallas kernels for 0%

commit v1 on v0

v1 whole, which is shorter than its diff:
```python
import functools
import math

import jax
import jax.numpy as jnp
import numpy as np
from jax import lax
from jax.experimental import pallas as pl
from jax.experimental.pallas import tpu as pltpu
from jax.sharding import PartitionSpec as P

SECTIONS = (16, 56, 56)
PH = 16
PW = 16
FRAME = PH * PW
HEAD_DIM = 128
ROPE_BASE = 256.0
NEG_FILL = -1e30
MESH = pl.DeviceIdType.MESH


def rope_tables(longest):
    angle_hw = np.zeros((FRAME, HEAD_DIM), np.float64)
    angle_t = np.zeros((longest, HEAD_DIM), np.float64)
    pairing = np.zeros((HEAD_DIM, HEAD_DIM), np.float32)
    row = np.arange(FRAME)
    first = 0
    for section, width in enumerate(SECTIONS):
        half = width // 2
        frequency = np.exp(-(2.0 * np.arange(half) / width) * math.log(ROPE_BASE))
        frequency = np.concatenate([frequency, frequency])
        lanes = slice(first, first + width)
        if section == 0:
            angle_t[:, lanes] = np.arange(longest)[:, None] * frequency[None, :]
        else:
            place = row // PW if section == 1 else row % PW
            angle_hw[:, lanes] = place[:, None] * frequency[None, :]
        for j in range(half):
            pairing[first + half + j, first + j] = -1.0
            pairing[first + j, first + half + j] = 1.0
        first += width
    angle_t = angle_t[:, None, :]
    tables = [np.cos(angle_hw), np.sin(angle_hw), np.cos(angle_t), np.sin(angle_t)]
    return [jnp.asarray(table, jnp.float32) for table in tables] + [
        jnp.asarray(pairing, jnp.bfloat16)
    ]


def clip_span(counts_ref, clips, longest, frame):
    start = jnp.int32(0)
    stop = jnp.int32(1 << 30)
    end = jnp.int32(0)
    for clip in range(clips):
        end = end + counts_ref[clip]
        start = jnp.where(end <= frame, end, start)
        stop = jnp.where(end > frame, jnp.minimum(stop, end), stop)
    return jnp.clip(start, frame - (longest - 1), frame), stop


def kernel(
    dims,
    counts_ref,
    q_ref,
    k_ref,
    v_ref,
    w_ref,
    cos_hw,
    sin_hw,
    cos_t,
    sin_t,
    pairing,
    out_ref,
    q_own,
    kv_own,
    q_all,
    kv_all,
    o_mine,
    o_all,
    w_all,
    total_ref,
    w_local,
    w_send,
    w_recv,
    kv_send,
    kv_recv,
    q_send,
    q_recv,
    halo_send,
    halo_recv,
    o_send,
    o_recv,
    x_send,
    x_recv,
):
    heads, group, groups, peers, slots, longest, clips, own_frames = dims
    rows = own_frames * FRAME
    halo = longest - 1
    span = group * own_frames
    reach = (halo + span - 1) // span
    columns = out_ref.shape[1]
    position = lax.axis_index("seq")
    tp = lax.axis_index("tp")
    plane = position // group
    member = position % group
    first_frame = plane * span

    def head_of(who, slot):
        return lax.rem(who - 2 * tp + 2 * group * peers, group) + slot * group

    def sized(slot):
        return min(group, heads - slot * group)

    def to_member(d):
        return lax.rem(member + d, group)

    def from_member(d):
        return lax.rem(member - d + group, group)

    def device(seq, core):
        return (seq, core)

    barrier = pltpu.get_barrier_semaphore()
    for d in range(1, group):
        pl.semaphore_signal(
            barrier, inc=1, device_id=device(plane * group + to_member(d), tp), device_id_type=MESH
        )
    for d in range(1, peers):
        pl.semaphore_signal(
            barrier, inc=1, device_id=device(position, lax.rem(tp + d, peers)), device_id_type=MESH
        )
    greeted = jnp.int32(group - 1 + peers - 1)
    for d in range(1, reach + 1):
        above = plane + d < groups
        below = plane - d >= 0

        @pl.when(above)
        def _():
            pl.semaphore_signal(
                barrier, inc=1, device_id=device(position + d * group, tp), device_id_type=MESH
            )

        @pl.when(below)
        def _():
            pl.semaphore_signal(
                barrier, inc=1, device_id=device(position - d * group, tp), device_id_type=MESH
            )

        greeted = greeted + above.astype(jnp.int32) + below.astype(jnp.int32)
    pl.semaphore_wait(barrier, greeted)

    lane = lax.broadcasted_iota(jnp.int32, (FRAME, HEAD_DIM), 1)
    in_t = lane < SECTIONS[0]
    cosines, sines = [], []
    for f in range(own_frames):
        frame = position * own_frames + f
        t = frame - clip_span(counts_ref, clips, longest, frame)[0]
        cosines.append(jnp.where(in_t, cos_t[t], cos_hw[...]))
        sines.append(jnp.where(in_t, sin_t[t], sin_hw[...]))

    def rotated(ref, f, head):
        x = ref[f * FRAME : (f + 1) * FRAME, head * HEAD_DIM : (head + 1) * HEAD_DIM]
        paired = jnp.dot(x, pairing[...], preferred_element_type=jnp.float32)
        return (x.astype(jnp.float32) * cosines[f] + paired * sines[f]).astype(jnp.bfloat16)

    def own_rows(who):
        return pl.ds(halo + who * own_frames, own_frames)

    def query_rows(who):
        return pl.ds(pl.multiple_of(who * rows, rows), rows)

    def kv_copy(slot, d, source, target):
        return pltpu.make_async_remote_copy(
            src_ref=kv_own.at[head_of(target, slot)],
            dst_ref=kv_all[slot].at[:, own_rows(source)],
            send_sem=kv_send.at[slot, d],
            recv_sem=kv_recv.at[slot, d],
            device_id=device(plane * group + target, tp),
            device_id_type=MESH,
        )

    def q_copy(slot, d, source, target):
        return pltpu.make_async_remote_copy(
            src_ref=q_own.at[head_of(target, slot)],
            dst_ref=q_all.at[slot, query_rows(source), :],
            send_sem=q_send.at[slot, d],
            recv_sem=q_recv.at[slot, d],
            device_id=device(plane * group + target, tp),
            device_id_type=MESH,
        )

    def o_copy(slot, d, source, target):
        return pltpu.make_async_remote_copy(
            src_ref=o_mine.at[slot, query_rows(target), :],
            dst_ref=o_all.at[tp, head_of(source, slot)],
            send_sem=o_send.at[slot, d],
            recv_sem=o_recv.at[slot, d],
            device_id=device(plane * group + target, tp),
            device_id_type=MESH,
        )

    def w_copy(d):
        target = lax.rem(tp + d, peers)
        return pltpu.make_async_remote_copy(
            src_ref=w_ref.at[:, pl.ds(pl.multiple_of(target * columns, columns), columns)],
            dst_ref=w_all.at[tp],
            send_sem=w_send.at[d],
            recv_sem=w_recv.at[d],
            device_id=device(position, target),
            device_id_type=MESH,
        )

    def w_arrival(d):
        source = lax.rem(tp - d + peers, peers)
        return pltpu.make_async_remote_copy(
            src_ref=w_ref.at[:, pl.ds(pl.multiple_of(tp * columns, columns), columns)],
            dst_ref=w_all.at[source],
            send_sem=w_send.at[d],
            recv_sem=w_recv.at[d],
            device_id=device(position, source),
            device_id_type=MESH,
        )

    def x_copy(slot, d, source, target):
        span_heads = pl.ds(slot * group, sized(slot))
        return pltpu.make_async_remote_copy(
            src_ref=o_all.at[source, span_heads],
            dst_ref=o_all.at[source, span_heads],
            send_sem=x_send.at[slot, d],
            recv_sem=x_recv.at[slot, d],
            device_id=device(position, target),
            device_id_type=MESH,
        )

    def halo_frames(d):
        return min(span, halo - span * (d - 1))

    def halo_copy(slot, d, upward, arriving):
        n = halo_frames(d)
        if upward:
            src_frame, dst_frame = halo + span - n, span - n - span * d + halo
        else:
            src_frame, dst_frame = halo, halo + span * d
        which = 2 * (d - 1) + (0 if upward else 1)
        away = d * group if upward != arriving else -d * group
        return pltpu.make_async_remote_copy(
            src_ref=kv_all[slot].at[:, pl.ds(src_frame, n)],
            dst_ref=kv_all[slot].at[:, pl.ds(dst_frame, n)],
            send_sem=halo_send.at[slot, which],
            recv_sem=halo_recv.at[slot, which],
            device_id=device(position + away, tp),
            device_id_type=MESH,
        )

    def exists(d, up):
        return plane + d < groups if up else plane - d >= 0

    have = [head_of(member, slot) < heads for slot in range(slots)]

    for slot in range(slots):
        span_heads = range(slot * group, slot * group + sized(slot))
        for head in span_heads:
            for f in range(own_frames):
                part = slice(f * FRAME, (f + 1) * FRAME)
                kv_own[head, 0, f] = rotated(k_ref, f, head)
                kv_own[head, 1, f] = v_ref[
                    part, head * HEAD_DIM : (head + 1) * HEAD_DIM
                ]
        for d in range(1, group):
            target = to_member(d)

            @pl.when(head_of(target, slot) < heads)
            def _():
                kv_copy(slot, d, member, target).start()

        for head in span_heads:
            for f in range(own_frames):
                part = slice(f * FRAME, (f + 1) * FRAME)
                q_own[head, part, :] = rotated(q_ref, f, head)
        for d in range(1, group):
            target = to_member(d)

            @pl.when(head_of(target, slot) < heads)
            def _():
                q_copy(slot, d, member, target).start()

    own_weight = pltpu.make_async_copy(
        w_ref.at[:, pl.ds(pl.multiple_of(tp * columns, columns), columns)],
        w_all.at[tp],
        w_local,
    )
    own_weight.start()
    for d in range(1, peers):
        w_copy(d).start()

    for slot in range(slots):

        @pl.when(have[slot])
        def _():
            mine = head_of(member, slot)
            kv_all[slot][:, own_rows(member)] = kv_own[mine]
            q_all[slot, query_rows(member), :] = q_own[mine]

            for d in range(1, reach + 1):
                for up in (True, False):

                    @pl.when(jnp.logical_not(exists(d, up)))
                    def _():
                        n = halo_frames(d)
                        blank = halo + span * d if up else span - n - span * d + halo
                        kv_all[slot][:, blank : blank + n] = jnp.zeros(
                            (2, n, FRAME, HEAD_DIM), jnp.bfloat16
                        )

            for d in range(1, group):
                kv_copy(slot, d, from_member(d), member).wait_recv()
            for d in range(1, reach + 1):
                for up in (True, False):

                    @pl.when(exists(d, up))
                    def _():
                        halo_copy(slot, d, up, False).start()

    scale = HEAD_DIM**-0.5 * math.log2(math.e)
    window = longest * FRAME
    column = lax.broadcasted_iota(jnp.int32, (1, window), 1)

    for slot in range(slots):

        @pl.when(have[slot])
        def _():
            mine = head_of(member, slot)
            for d in range(1, group):
                q_copy(slot, d, from_member(d), member).wait_recv()
            for d in range(1, reach + 1):
                for up in (True, False):

                    @pl.when(exists(d, not up))
                    def _():
                        halo_copy(slot, d, up, True).wait_recv()

            def attend(step, carry):
                d = lax.rem(step + 1, group)
                target = to_member(d)
                for f in range(own_frames):
                    place = target * own_frames + f
                    start, stop = clip_span(counts_ref, clips, longest, first_frame + place)
                    here = pl.ds(pl.multiple_of(place * FRAME, FRAME), FRAME)
                    first_key = start - first_frame + halo
                    keys = jnp.concatenate(
                        [kv_all[slot][0, first_key + i] for i in range(longest)], axis=0
                    )
                    values = jnp.concatenate(
                        [kv_all[slot][1, first_key + i] for i in range(longest)], axis=0
                    )
                    scores = lax.dot_general(
                        q_all[slot, here, :],
                        keys,
                        (((1,), (1,)), ((), ())),
                        preferred_element_type=jnp.float32,
                    )
                    scores = jnp.where(column < (stop - start) * FRAME, scores, NEG_FILL)
                    largest = jnp.max(scores, axis=1, keepdims=True)
                    expo = jnp.exp2((scores - largest) * scale)
                    total = jnp.sum(expo, axis=1, keepdims=True)
                    summed = jnp.dot(
                        expo.astype(jnp.bfloat16), values, preferred_element_type=jnp.float32
                    )
                    o_mine[slot, here, :] = (summed / total).astype(jnp.bfloat16)

                @pl.when(d > 0)
                def _():
                    o_copy(slot, d, member, target).start()

                return carry

            lax.fori_loop(0, group, attend, 0)
            o_all[tp, mine] = o_mine[slot, query_rows(member), :]

    for slot in range(slots):
        for d in range(1, group):
            source = from_member(d)

            @pl.when(head_of(source, slot) < heads)
            def _():
                o_copy(slot, d, source, member).wait_recv()

        for d in range(1, peers):
            x_copy(slot, d, tp, lax.rem(tp + d, peers)).start()

    chunk = 256
    own_weight.wait()

    def project(source, into, last):
        left = jnp.concatenate([o_all[source, head] for head in range(heads)], axis=1)

        def body(step, carry):
            place = pl.ds(pl.multiple_of(step * chunk, chunk), chunk)
            term = jnp.dot(left, w_all[source, :, place], preferred_element_type=jnp.float32)
            if into:
                term = total_ref[:, place] + term
            if last:
                out_ref[:, place] = term.astype(jnp.bfloat16)
            else:
                total_ref[:, place] = term
            return carry

        lax.fori_loop(0, columns // chunk, body, 0)

    project(tp, False, peers == 1)
    for d in range(1, peers):
        source = lax.rem(tp - d + peers, peers)
        w_arrival(d).wait_recv()
        for slot in range(slots):
            x_copy(slot, d, source, tp).wait_recv()
        project(source, True, d == peers - 1)

    for d in range(1, peers):
        w_copy(d).wait_send()
    for slot in range(slots):
        for d in range(1, peers):
            x_copy(slot, d, tp, lax.rem(tp + d, peers)).wait_send()
        for d in range(1, group):
            target = to_member(d)

            @pl.when(head_of(target, slot) < heads)
            def _():
                kv_copy(slot, d, member, target).wait_send()
                q_copy(slot, d, member, target).wait_send()

            @pl.when(have[slot])
            def _():
                o_copy(slot, d, member, target).wait_send()

        for d in range(1, reach + 1):
            for up in (True, False):

                @pl.when(have[slot] & exists(d, up))
                def _():
                    halo_copy(slot, d, up, False).wait_send()


def per_device(seq, peers, query_rows, key_rows, value_rows, frame_counts, out_weight):
    rows, features = query_rows.shape
    heads = features // HEAD_DIM
    own_frames = rows // FRAME
    longest = own_frames * seq // 8
    group = 4
    groups = seq // group
    slots = -(-heads // group)
    columns = out_weight.shape[1] // peers
    clips = frame_counts.shape[0]
    span = group * own_frames
    halo = longest - 1
    reach = -(-halo // span)
    dims = (heads, group, groups, peers, slots, longest, clips, own_frames)
    vmem = pl.BlockSpec(memory_space=pltpu.VMEM)
    dma = pltpu.SemaphoreType.DMA
    bf16 = jnp.bfloat16
    flops = 2 * rows * features * out_weight.shape[1]
    return pl.pallas_call(
        functools.partial(kernel, dims),
        out_shape=jax.ShapeDtypeStruct((rows, columns), bf16),
        in_specs=[
            pl.BlockSpec(memory_space=pltpu.SMEM),
            vmem,
            vmem,
            vmem,
            pl.BlockSpec(memory_space=pl.ANY),
        ]
        + [vmem] * 5,
        out_specs=vmem,
        scratch_shapes=[
            pltpu.VMEM((heads, rows, HEAD_DIM), bf16),
            pltpu.VMEM((heads, 2, own_frames, FRAME, HEAD_DIM), bf16),
            pltpu.VMEM((slots, group * rows, HEAD_DIM), bf16),
            [pltpu.VMEM((2, span + 2 * halo, FRAME, HEAD_DIM), bf16)] * slots,
            pltpu.VMEM((slots, group * rows, HEAD_DIM), bf16),
            pltpu.VMEM((peers, heads, rows, HEAD_DIM), bf16),
            pltpu.VMEM((peers, features, columns), bf16),
            pltpu.VMEM((rows, columns), jnp.float32),
            dma(()),
            dma((peers,)),
            dma((peers,)),
            dma((slots, group)),
            dma((slots, group)),
            dma((slots, group)),
            dma((slots, group)),
            dma((slots, 2 * reach)),
            dma((slots, 2 * reach)),
            dma((slots, group)),
            dma((slots, group)),
            dma((slots, peers)),
            dma((slots, peers)),
        ],
        compiler_params=pltpu.CompilerParams(
            collective_id=0, has_side_effects=True, vmem_limit_bytes=56 * 1024 * 1024
        ),
        cost_estimate=pl.CostEstimate(flops=flops, bytes_accessed=8 << 20, transcendentals=0),
    )(frame_counts, query_rows, key_rows, value_rows, out_weight, *rope_tables(longest))


def solution(mesh):
    return jax.shard_map(
        functools.partial(per_device, mesh.shape["seq"], mesh.shape["tp"]),
        mesh=mesh,
        in_specs=(P("seq", "tp"), P("seq", "tp"), P("seq", "tp"), P(), P("tp", None)),
        out_specs=P("seq", "tp"),
        check_vma=False,
    )
```

time: 311 us -> 55.2 us (0.18)
  waiting for transfers between devices: 185 us -> 0 us
  Pallas kernels: 0 us -> 52.4 us
  local copies, waits for them, and re-layouts: 50.4 us -> 2.65 us
  matrix products: 27.4 us -> 0 us
  other arithmetic: 26.1 us -> 0 us
  between operations: 13.7 us -> 0.01 us
  starting transfers between devices: 7.51 us -> 0 us
    ppermute x5 -> x0, waiting for transfers between devices: 178 us -> none  [from_behind(): lax.ppermute(value, axis, [(i, (i + by) % count) for i in range(count)])]
    pallas_call x0 -> x1, Pallas kernels: none -> 52.4 us  [per_device(): pl.pallas_call(functools.partial(kernel, dims), out_shape=jax.ShapeDtypeS...]
    dot_general x11 -> x0, matrix products: 27.4 us -> none  [the longest x5 14.5 us: absorb(): jnp.einsum('hts,shd->htd', expo.astype(jnp.bfloat16), value_heads, prefer...]
    unnamed x55 -> x1, local copies, waits for them, and re-layouts: 25 us -> 2.65 us
    another operation x11 -> x0, other arithmetic: 12.2 us -> none
    concatenate x3 -> x0, local copies, waits for them, and re-layouts: 11.3 us -> none  [rotate(): return jnp.concatenate(pieces, axis=2)]
    while x25 -> x0, local copies, waits for them, and re-layouts: 8.53 us -> none
    reduce_sum x10 -> x0, other arithmetic: 8.03 us -> none  [the longest x5 7.57 us: absorb(): run_total = run_total * rescale + jnp.sum(expo, axis=2)]
  transfers between devices with their start and end apart: 6 -> 0, of which waited for: 6 -> 0; matrix products, arithmetic and copies ran while one was open for 2% -> 0% of each run, Pallas kernels for 0% -> 0%
where the time goes in v1:
time: 55.2 us; the launch traced here: 55.1 us
  Pallas kernels  52.4 us (95%)
  local copies, waits for them, and re-layouts  2.65 us (5%)
    pallas_call x1, Pallas kernels, per_device(): pl.pallas_call(functools.partial(kernel, dims), out_shape=jax.ShapeDtypeS...  52.4 us
    unnamed x1, local copies, waits for them, and re-layouts  2.65 us

profile of v1, /device:TPU:0, one launch (start us, length us, event | category | flops | bytes accessed | tf_op | source)
XLA Modules:
  0.0 55.1 jit_solution(8016841931013859355)
XLA Ops:
  0.0 52.4 %shard_map.100 = bf16[512,1536]{1,0:T(8,128)(2,1)} custom-call(s32[12]{0:T(128)} %counts_ref.1, bf16[512,768]{1,0:T(8,128)(2,1)} %q_ref.1, bf16[512,768]{1,0:T(8,128)(2,1)} %k_ref.1, bf16[512,768]{1,0:T(8,128)(2,1)} %v_ref.1, bf16[768,3072]{1,0:T(8,128)(2,1)} %w_ref.1, f32[256,128]{1,0:T(8,128)} %constant.10.clone.cos_hw, f32[256,128]{1,0:T(8,128)} %constant.11.clone.sin_hw, ...), custom_call_target="tpu_custom_call" | custom-call | flops 2415919104 | bytes 8388608 | tf_op jit(solution)/shard_map/pallas_call | solution.py:460
  52.4 2.7 %copy.12 = bf16[512,1536]{1,0:T(8,128)(2,1)} copy(bf16[512,1536]{1,0:T(8,128)(2,1)} %shard_map.100) | data formatting | bytes 3145728

commit v2 on v1

--- a/solution.py
+++ b/solution.py
@@ -70,19 +70,26 @@
     sin_t,
     pairing,
     out_ref,
+    q_in,
+    k_in,
     q_own,
-    kv_own,
+    k_own,
     q_all,
-    kv_all,
+    k_all,
+    v_all,
     o_mine,
     o_all,
     w_all,
     total_ref,
+    in_local,
     w_local,
+    v_local,
     w_send,
     w_recv,
-    kv_send,
-    kv_recv,
+    k_send,
+    k_recv,
+    v_send,
+    v_recv,
     q_send,
     q_recv,
     halo_send,
@@ -119,6 +126,13 @@
     def device(seq, core):
         return (seq, core)
 
+    loads = [
+        pltpu.make_async_copy(k_ref, k_in, in_local.at[0]),
+        pltpu.make_async_copy(q_ref, q_in, in_local.at[1]),
+    ]
+    for load in loads:
+        load.start()
+
     barrier = pltpu.get_barrier_semaphore()
     for d in range(1, group):
         pl.semaphore_signal(
@@ -168,14 +182,34 @@
     def query_rows(who):
         return pl.ds(pl.multiple_of(who * rows, rows), rows)
 
-    def kv_copy(slot, d, source, target):
-        return pltpu.make_async_remote_copy(
-            src_ref=kv_own.at[head_of(target, slot)],
-            dst_ref=kv_all[slot].at[:, own_rows(source)],
-            send_sem=kv_send.at[slot, d],
-            recv_sem=kv_recv.at[slot, d],
+    def lanes_of(head):
+        return pl.ds(pl.multiple_of(head * HEAD_DIM, HEAD_DIM), HEAD_DIM)
+
+    def k_copy(slot, d, source, target):
+        return pltpu.make_async_remote_copy(
+            src_ref=k_own.at[head_of(target, slot)],
+            dst_ref=k_all[slot].at[own_rows(source)],
+            send_sem=k_send.at[slot, d],
+            recv_sem=k_recv.at[slot, d],
             device_id=device(plane * group + target, tp),
             device_id_type=MESH,
+        )
+
+    def v_copy(slot, d, source, target):
+        return pltpu.make_async_remote_copy(
+            src_ref=v_ref.at[:, :, lanes_of(head_of(target, slot))],
+            dst_ref=v_all[slot].at[own_rows(source)],
+            send_sem=v_send.at[slot, d],
+            recv_sem=v_recv.at[slot, d],
+            device_id=device(plane * group + target, tp),
+            device_id_type=MESH,
+        )
+
+    def v_stay(slot):
+        return pltpu.make_async_copy(
+            v_ref.at[:, :, lanes_of(head_of(member, slot))],
+            v_all[slot].at[own_rows(member)],
+            v_local.at[slot],
         )
 
     def q_copy(slot, d, source, target):
@@ -234,7 +268,7 @@
     def halo_frames(d):
         return min(span, halo - span * (d - 1))
 
-    def halo_copy(slot, d, upward, arriving):
+    def halo_copy(slot, what, d, upward, arriving):
         n = halo_frames(d)
         if upward:
             src_frame, dst_frame = halo + span - n, span - n - span * d + halo
@@ -242,11 +276,12 @@
             src_frame, dst_frame = halo, halo + span * d
         which = 2 * (d - 1) + (0 if upward else 1)
         away = d * group if upward != arriving else -d * group
-        return pltpu.make_async_remote_copy(
-            src_ref=kv_all[slot].at[:, pl.ds(src_frame, n)],
-            dst_ref=kv_all[slot].at[:, pl.ds(dst_frame, n)],
-            send_sem=halo_send.at[slot, which],
-            recv_sem=halo_recv.at[slot, which],
+        buffer = (k_all, v_all)[what][slot]
+        return pltpu.make_async_remote_copy(
+            src_ref=buffer.at[pl.ds(src_frame, n)],
+            dst_ref=buffer.at[pl.ds(dst_frame, n)],
+            send_sem=halo_send.at[slot, what, which],
+            recv_sem=halo_recv.at[slot, what, which],
             device_id=device(position + away, tp),
             device_id_type=MESH,
         )
@@ -256,147 +291,176 @@
 
     have = [head_of(member, slot) < heads for slot in range(slots)]
 
-    for slot in range(slots):
-        span_heads = range(slot * group, slot * group + sized(slot))
-        for head in span_heads:
-            for f in range(own_frames):
-                part = slice(f * FRAME, (f + 1) * FRAME)
-                kv_own[head, 0, f] = rotated(k_ref, f, head)
-                kv_own[head, 1, f] = v_ref[
-                    part, head * HEAD_DIM : (head + 1) * HEAD_DIM
-                ]
+    def send(copy, slot):
         for d in range(1, group):
             target = to_member(d)
 
             @pl.when(head_of(target, slot) < heads)
             def _():
-                kv_copy(slot, d, member, target).start()
-
-        for head in span_heads:
-            for f in range(own_frames):
-                part = slice(f * FRAME, (f + 1) * FRAME)
-                q_own[head, part, :] = rotated(q_ref, f, head)
-        for d in range(1, group):
-            target = to_member(d)
-
-            @pl.when(head_of(target, slot) < heads)
-            def _():
-                q_copy(slot, d, member, target).start()
+                copy(slot, d, member, target).start()
 
     own_weight = pltpu.make_async_copy(
         w_ref.at[:, pl.ds(pl.multiple_of(tp * columns, columns), columns)],
         w_all.at[tp],
         w_local,
     )
-    own_weight.start()
-    for d in range(1, peers):
-        w_copy(d).start()
 
     for slot in range(slots):
+        slot_heads = range(slot * group, slot * group + sized(slot))
+        send(v_copy, slot)
 
         @pl.when(have[slot])
         def _():
-            mine = head_of(member, slot)
-            kv_all[slot][:, own_rows(member)] = kv_own[mine]
-            q_all[slot, query_rows(member), :] = q_own[mine]
-
+            v_stay(slot).start()
+
+        if slot == 0:
+            loads[0].wait()
+        for head in slot_heads:
+            for f in range(own_frames):
+                k_own[head, f] = rotated(k_in, f, head)
+        send(k_copy, slot)
+        if slot == 0:
+            loads[1].wait()
+        for head in slot_heads:
+            for f in range(own_frames):
+                part = slice(f * FRAME, (f + 1) * FRAME)
+                q_own[head, part, :] = rotated(q_in, f, head)
+        send(q_copy, slot)
+        if slot == 0:
+            own_weight.start()
+            for d in range(1, peers):
+                w_copy(d).start()
+
+    scale = HEAD_DIM**-0.5 * math.log2(math.e)
+
+    def start_halos(slot, what):
+        for d in range(1, reach + 1):
+            for up in (True, False):
+
+                @pl.when(exists(d, up))
+                def _():
+                    halo_copy(slot, what, d, up, False).start()
+
+    def spread(slot):
+        mine = head_of(member, slot)
+        k_all[slot][own_rows(member)] = k_own[mine]
+        q_all[slot, query_rows(member), :] = q_own[mine]
+        for d in range(1, reach + 1):
+            for up in (True, False):
+
+                @pl.when(jnp.logical_not(exists(d, up)))
+                def _():
+                    n = halo_frames(d)
+                    blank = halo + span * d if up else span - n - span * d + halo
+                    for buffer in (k_all, v_all):
+                        buffer[slot][blank : blank + n] = jnp.zeros(
+                            (n, FRAME, HEAD_DIM), jnp.bfloat16
+                        )
+
+        v_stay(slot).wait()
+        for d in range(1, group):
+            v_copy(slot, d, from_member(d), member).wait_recv()
+        start_halos(slot, 1)
+        for d in range(1, group):
+            k_copy(slot, d, from_member(d), member).wait_recv()
+        start_halos(slot, 0)
+
+    def settle(slot):
+        for d in range(1, group):
+            q_copy(slot, d, from_member(d), member).wait_recv()
+        for what in (1, 0):
             for d in range(1, reach + 1):
                 for up in (True, False):
 
-                    @pl.when(jnp.logical_not(exists(d, up)))
-                    def _():
-                        n = halo_frames(d)
-                        blank = halo + span * d if up else span - n - span * d + halo
-                        kv_all[slot][:, blank : blank + n] = jnp.zeros(
-                            (2, n, FRAME, HEAD_DIM), jnp.bfloat16
-                        )
-
-            for d in range(1, group):
-                kv_copy(slot, d, from_member(d), member).wait_recv()
-            for d in range(1, reach + 1):
-                for up in (True, False):
-
-                    @pl.when(exists(d, up))
-                    def _():
-                        halo_copy(slot, d, up, False).start()
-
-    scale = HEAD_DIM**-0.5 * math.log2(math.e)
-    window = longest * FRAME
-    column = lax.broadcasted_iota(jnp.int32, (1, window), 1)
-
-    for slot in range(slots):
-
-        @pl.when(have[slot])
-        def _():
-            mine = head_of(member, slot)
-            for d in range(1, group):
-                q_copy(slot, d, from_member(d), member).wait_recv()
-            for d in range(1, reach + 1):
-                for up in (True, False):
-
                     @pl.when(exists(d, not up))
                     def _():
-                        halo_copy(slot, d, up, True).wait_recv()
-
-            def attend(step, carry):
-                d = lax.rem(step + 1, group)
-                target = to_member(d)
-                for f in range(own_frames):
-                    place = target * own_frames + f
-                    start, stop = clip_span(counts_ref, clips, longest, first_frame + place)
-                    here = pl.ds(pl.multiple_of(place * FRAME, FRAME), FRAME)
-                    first_key = start - first_frame + halo
-                    keys = jnp.concatenate(
-                        [kv_all[slot][0, first_key + i] for i in range(longest)], axis=0
-                    )
-                    values = jnp.concatenate(
-                        [kv_all[slot][1, first_key + i] for i in range(longest)], axis=0
-                    )
-                    scores = lax.dot_general(
-                        q_all[slot, here, :],
-                        keys,
-                        (((1,), (1,)), ((), ())),
-                        preferred_element_type=jnp.float32,
-                    )
-                    scores = jnp.where(column < (stop - start) * FRAME, scores, NEG_FILL)
-                    largest = jnp.max(scores, axis=1, keepdims=True)
-                    expo = jnp.exp2((scores - largest) * scale)
-                    total = jnp.sum(expo, axis=1, keepdims=True)
-                    summed = jnp.dot(
-                        expo.astype(jnp.bfloat16), values, preferred_element_type=jnp.float32
-                    )
-                    o_mine[slot, here, :] = (summed / total).astype(jnp.bfloat16)
-
-                @pl.when(d > 0)
-                def _():
-                    o_copy(slot, d, member, target).start()
-
-                return carry
-
-            lax.fori_loop(0, group, attend, 0)
-            o_all[tp, mine] = o_mine[slot, query_rows(member), :]
-
-    for slot in range(slots):
-        for d in range(1, group):
-            source = from_member(d)
-
-            @pl.when(head_of(source, slot) < heads)
+                        halo_copy(slot, what, d, up, True).wait_recv()
+
+    ones = jnp.ones((FRAME, HEAD_DIM), jnp.bfloat16)
+
+    def attend(slot, step, carry):
+        d = lax.rem(step + 1, group)
+        target = to_member(d)
+        for f in range(own_frames):
+            place = target * own_frames + f
+            start, stop = clip_span(counts_ref, clips, longest, first_frame + place)
+            here = pl.ds(pl.multiple_of(place * FRAME, FRAME), FRAME)
+            first_key = start - first_frame + halo
+            queries = q_all[slot, here, :]
+            scores, tops, values, inside = [], [], [], []
+            largest = None
+            for i in range(longest):
+                part = lax.dot_general(
+                    queries,
+                    k_all[slot][first_key + i],
+                    (((1,), (1,)), ((), ())),
+                    preferred_element_type=jnp.float32,
+                )
+                top = jnp.max(part, axis=1, keepdims=True)
+                same = jnp.full((FRAME, 1), start + i, jnp.int32) < stop
+                kept = jnp.where(same, top, NEG_FILL)
+                largest = kept if i == 0 else jnp.maximum(largest, kept)
+                both = jnp.concatenate([v_all[slot][first_key + i], ones], axis=1)
+                in_clip = jnp.full(both.shape, start + i, jnp.int32) < stop
+                scores.append(part)
+                tops.append(top)
+                inside.append(same)
+                values.append(jnp.where(in_clip, both, jnp.zeros_like(both)))
+            weights = [
+                jnp.exp2((part - jnp.where(same, largest, top)) * scale).astype(jnp.bfloat16)
+                for part, same, top in zip(scores, inside, tops)
+            ]
+            summed = jnp.dot(
+                jnp.concatenate(weights, axis=1),
+                jnp.concatenate(values, axis=0),
+                preferred_element_type=jnp.float32,
+            )
+            o_mine[slot, here, :] = (
+                summed[:, :HEAD_DIM] / summed[:, HEAD_DIM:]
+            ).astype(jnp.bfloat16)
+
+        @pl.when(d > 0)
+        def _():
+            o_copy(slot, d, member, target).start()
+
+        return carry
+
+    @pl.when(have[0])
+    def _():
+        spread(0)
+        settle(0)
+        lax.fori_loop(0, group // 2, functools.partial(attend, 0), 0)
+
+    for slot in range(1, slots + 1):
+        if slot < slots:
+
+            @pl.when(have[slot])
             def _():
-                o_copy(slot, d, source, member).wait_recv()
-
-        for d in range(1, peers):
-            x_copy(slot, d, tp, lax.rem(tp + d, peers)).start()
+                spread(slot)
+
+        @pl.when(have[slot - 1])
+        def _():
+            lax.fori_loop(group // 2, group, functools.partial(attend, slot - 1), 0)
+            o_all[tp, head_of(member, slot - 1)] = o_mine[slot - 1, query_rows(member), :]
+
+        if slot < slots:
+
+            @pl.when(have[slot])
+            def _():
+                settle(slot)
+                lax.fori_loop(0, group // 2, functools.partial(attend, slot), 0)
 
     chunk = 256
-    own_weight.wait()
-
-    def project(source, into, last):
-        left = jnp.concatenate([o_all[source, head] for head in range(heads)], axis=1)
+
+    def project(source, slot, first, last):
+        slot_heads = range(slot * group, slot * group + sized(slot))
+        left = jnp.concatenate([o_all[source, head] for head in slot_heads], axis=1)
+        deep = slice(slot * group * HEAD_DIM, (slot * group + sized(slot)) * HEAD_DIM)
 
         def body(step, carry):
             place = pl.ds(pl.multiple_of(step * chunk, chunk), chunk)
-            term = jnp.dot(left, w_all[source, :, place], preferred_element_type=jnp.float32)
-            if into:
+            term = jnp.dot(left, w_all[source, deep, place], preferred_element_type=jnp.float32)
+            if not first:
                 term = total_ref[:, place] + term
             if last:
                 out_ref[:, place] = term.astype(jnp.bfloat16)
@@ -406,13 +470,26 @@
 
         lax.fori_loop(0, columns // chunk, body, 0)
 
-    project(tp, False, peers == 1)
+    own_weight.wait()
+    for slot in range(slots):
+        for d in range(1, group):
+            source = from_member(d)
+
+            @pl.when(head_of(source, slot) < heads)
+            def _():
+                o_copy(slot, d, source, member).wait_recv()
+
+        for d in range(1, peers):
+            x_copy(slot, d, tp, lax.rem(tp + d, peers)).start()
+        project(tp, slot, slot == 0, peers == 1 and slot == slots - 1)
+
     for d in range(1, peers):
-        source = lax.rem(tp - d + peers, peers)
         w_arrival(d).wait_recv()
-        for slot in range(slots):
+    for slot in range(slots):
+        for d in range(1, peers):
+            source = lax.rem(tp - d + peers, peers)
             x_copy(slot, d, source, tp).wait_recv()
-        project(source, True, d == peers - 1)
+            project(source, slot, False, slot == slots - 1 and d == peers - 1)
 
     for d in range(1, peers):
         w_copy(d).wait_send()
@@ -424,7 +501,8 @@
 
             @pl.when(head_of(target, slot) < heads)
             def _():
-                kv_copy(slot, d, member, target).wait_send()
+                k_copy(slot, d, member, target).wait_send()
+                v_copy(slot, d, member, target).wait_send()
                 q_copy(slot, d, member, target).wait_send()
 
             @pl.when(have[slot])
@@ -436,7 +514,8 @@
 
                 @pl.when(have[slot] & exists(d, up))
                 def _():
-                    halo_copy(slot, d, up, False).wait_send()
+                    for what in (0, 1):
+                        halo_copy(slot, what, d, up, False).wait_send()
 
 
 def per_device(seq, peers, query_rows, key_rows, value_rows, frame_counts, out_weight):
@@ -453,6 +532,7 @@
     halo = longest - 1
     reach = -(-halo // span)
     dims = (heads, group, groups, peers, slots, longest, clips, own_frames)
+    value_frames = value_rows.reshape(own_frames, FRAME, features)
     vmem = pl.BlockSpec(memory_space=pltpu.VMEM)
     dma = pltpu.SemaphoreType.DMA
     bf16 = jnp.bfloat16
@@ -462,31 +542,35 @@
         out_shape=jax.ShapeDtypeStruct((rows, columns), bf16),
         in_specs=[
             pl.BlockSpec(memory_space=pltpu.SMEM),
-            vmem,
-            vmem,
-            vmem,
-            pl.BlockSpec(memory_space=pl.ANY),
         ]
+        + [pl.BlockSpec(memory_space=pl.ANY)] * 4
         + [vmem] * 5,
         out_specs=vmem,
         scratch_shapes=[
+            pltpu.VMEM((rows, features), bf16),
+            pltpu.VMEM((rows, features), bf16),
             pltpu.VMEM((heads, rows, HEAD_DIM), bf16),
-            pltpu.VMEM((heads, 2, own_frames, FRAME, HEAD_DIM), bf16),
+            pltpu.VMEM((heads, own_frames, FRAME, HEAD_DIM), bf16),
             pltpu.VMEM((slots, group * rows, HEAD_DIM), bf16),
-            [pltpu.VMEM((2, span + 2 * halo, FRAME, HEAD_DIM), bf16)] * slots,
+            [pltpu.VMEM((span + 2 * halo, FRAME, HEAD_DIM), bf16)] * slots,
+            [pltpu.VMEM((span + 2 * halo, FRAME, HEAD_DIM), bf16)] * slots,
             pltpu.VMEM((slots, group * rows, HEAD_DIM), bf16),
             pltpu.VMEM((peers, heads, rows, HEAD_DIM), bf16),
             pltpu.VMEM((peers, features, columns), bf16),
             pltpu.VMEM((rows, columns), jnp.float32),
+            dma((2,)),
             dma(()),
+            dma((slots,)),
             dma((peers,)),
             dma((peers,)),
             dma((slots, group)),
             dma((slots, group)),
             dma((slots, group)),
             dma((slots, group)),
-            dma((slots, 2 * reach)),
-            dma((slots, 2 * reach)),
+            dma((slots, group)),
+            dma((slots, group)),
+            dma((slots, 2, 2 * reach)),
+            dma((slots, 2, 2 * reach)),
             dma((slots, group)),
             dma((slots, group)),
             dma((slots, peers)),
@@ -496,7 +580,7 @@
             collective_id=0, has_side_effects=True, vmem_limit_bytes=56 * 1024 * 1024
         ),
         cost_estimate=pl.CostEstimate(flops=flops, bytes_accessed=8 << 20, transcendentals=0),
-    )(frame_counts, query_rows, key_rows, value_rows, out_weight, *rope_tables(longest))
+    )(frame_counts, query_rows, key_rows, value_frames, out_weight, *rope_tables(longest))
 
 
 def solution(mesh):

time: 55.2 us -> 52.7 us (0.955)
  Pallas kernels: 52.4 us -> 49.9 us
    pallas_call x1, Pallas kernels: 52.4 us -> 49.9 us  [per_device(): pl.pallas_call(functools.partial(kernel, dims), out_shape=jax.ShapeDtypeS...]
where the time goes in v2:
time: 52.7 us; the launch traced here: 52.5 us
  Pallas kernels  49.9 us (95%)
  local copies, waits for them, and re-layouts  2.65 us (5%)
    pallas_call x1, Pallas kernels, per_device(): pl.pallas_call(functools.partial(kernel, dims), out_shape=jax.ShapeDtypeS...  49.9 us
    unnamed x1, local copies, waits for them, and re-layouts  2.65 us

profile of v2, /device:TPU:0, one launch (start us, length us, event | category | flops | bytes accessed | tf_op | source)
XLA Modules:
  0.0 52.5 jit_solution(4001548975153047121)
XLA Ops:
  0.0 49.9 %shard_map.100 = bf16[512,1536]{1,0:T(8,128)(2,1)} custom-call(s32[12]{0:T(128)} %counts_ref.1, bf16[512,768]{1,0:T(8,128)(2,1)} %q_ref.1, bf16[512,768]{1,0:T(8,128)(2,1)} %k_ref.1, bf16[2,256,768]{2,1,0:T(8,128)(2,1)} %bitcast.1, bf16[768,3072]{1,0:T(8,128)(2,1)} %w_ref.1, f32[256,128]{1,0:T(8,128)} %constant.10.clone.cos_hw, ...), custom_call_target="tpu_custom_call" | custom-call | flops 2415919104 | bytes 8388608 | tf_op jit(solution)/shard_map/pallas_call | solution.py:540
  49.9 2.7 %copy.12 = bf16[512,1536]{1,0:T(8,128)(2,1)} copy(bf16[512,1536]{1,0:T(8,128)(2,1)} %shard_map.100) | data formatting | bytes 3145728

commit v3 on v2

--- a/solution.py
+++ b/solution.py
@@ -64,14 +64,19 @@
     k_ref,
     v_ref,
     w_ref,
+    cos_hw_ref,
+    sin_hw_ref,
+    cos_t_ref,
+    sin_t_ref,
+    pairing_ref,
+    out_ref,
+    q_in,
+    k_in,
     cos_hw,
     sin_hw,
     cos_t,
     sin_t,
     pairing,
-    out_ref,
-    q_in,
-    k_in,
     q_own,
     k_own,
     q_all,
@@ -127,8 +132,18 @@
         return (seq, core)
 
     loads = [
-        pltpu.make_async_copy(k_ref, k_in, in_local.at[0]),
-        pltpu.make_async_copy(q_ref, q_in, in_local.at[1]),
+        pltpu.make_async_copy(source, target, in_local.at[i])
+        for i, (source, target) in enumerate(
+            [
+                (cos_hw_ref, cos_hw),
+                (sin_hw_ref, sin_hw),
+                (cos_t_ref, cos_t),
+                (sin_t_ref, sin_t),
+                (pairing_ref, pairing),
+                (k_ref, k_in),
+                (q_ref, q_in),
+            ]
+        )
     ]
     for load in loads:
         load.start()
@@ -162,14 +177,7 @@
         greeted = greeted + above.astype(jnp.int32) + below.astype(jnp.int32)
     pl.semaphore_wait(barrier, greeted)
 
-    lane = lax.broadcasted_iota(jnp.int32, (FRAME, HEAD_DIM), 1)
-    in_t = lane < SECTIONS[0]
     cosines, sines = [], []
-    for f in range(own_frames):
-        frame = position * own_frames + f
-        t = frame - clip_span(counts_ref, clips, longest, frame)[0]
-        cosines.append(jnp.where(in_t, cos_t[t], cos_hw[...]))
-        sines.append(jnp.where(in_t, sin_t[t], sin_hw[...]))
 
     def rotated(ref, f, head):
         x = ref[f * FRAME : (f + 1) * FRAME, head * HEAD_DIM : (head + 1) * HEAD_DIM]
@@ -291,6 +299,15 @@
 
     have = [head_of(member, slot) < heads for slot in range(slots)]
 
+    def angles():
+        lane = lax.broadcasted_iota(jnp.int32, (FRAME, HEAD_DIM), 1)
+        in_t = lane < SECTIONS[0]
+        for f in range(own_frames):
+            frame = position * own_frames + f
+            t = frame - clip_span(counts_ref, clips, longest, frame)[0]
+            cosines.append(jnp.where(in_t, cos_t[t], cos_hw[...]))
+            sines.append(jnp.where(in_t, sin_t[t], sin_hw[...]))
+
     def send(copy, slot):
         for d in range(1, group):
             target = to_member(d)
@@ -314,22 +331,20 @@
             v_stay(slot).start()
 
         if slot == 0:
-            loads[0].wait()
+            for load in loads[:-1]:
+                load.wait()
+            angles()
         for head in slot_heads:
             for f in range(own_frames):
                 k_own[head, f] = rotated(k_in, f, head)
         send(k_copy, slot)
         if slot == 0:
-            loads[1].wait()
+            loads[-1].wait()
         for head in slot_heads:
             for f in range(own_frames):
                 part = slice(f * FRAME, (f + 1) * FRAME)
                 q_own[head, part, :] = rotated(q_in, f, head)
         send(q_copy, slot)
-        if slot == 0:
-            own_weight.start()
-            for d in range(1, peers):
-                w_copy(d).start()
 
     scale = HEAD_DIM**-0.5 * math.log2(math.e)
 
@@ -431,6 +446,10 @@
         settle(0)
         lax.fori_loop(0, group // 2, functools.partial(attend, 0), 0)
 
+    own_weight.start()
+    for d in range(1, peers):
+        w_copy(d).start()
+
     for slot in range(1, slots + 1):
         if slot < slots:
 
@@ -543,12 +562,16 @@
         in_specs=[
             pl.BlockSpec(memory_space=pltpu.SMEM),
         ]
-        + [pl.BlockSpec(memory_space=pl.ANY)] * 4
-        + [vmem] * 5,
+        + [pl.BlockSpec(memory_space=pltpu.HBM)] * 9,
         out_specs=vmem,
         scratch_shapes=[
             pltpu.VMEM((rows, features), bf16),
             pltpu.VMEM((rows, features), bf16),
+            pltpu.VMEM((FRAME, HEAD_DIM), jnp.float32),
+            pltpu.VMEM((FRAME, HEAD_DIM), jnp.float32),
+            pltpu.VMEM((longest, 1, HEAD_DIM), jnp.float32),
+            pltpu.VMEM((longest, 1, HEAD_DIM), jnp.float32),
+            pltpu.VMEM((HEAD_DIM, HEAD_DIM), bf16),
             pltpu.VMEM((heads, rows, HEAD_DIM), bf16),
             pltpu.VMEM((heads, own_frames, FRAME, HEAD_DIM), bf16),
             pltpu.VMEM((slots, group * rows, HEAD_DIM), bf16),
@@ -558,7 +581,7 @@
             pltpu.VMEM((peers, heads, rows, HEAD_DIM), bf16),
             pltpu.VMEM((peers, features, columns), bf16),
             pltpu.VMEM((rows, columns), jnp.float32),
-            dma((2,)),
+            dma((7,)),
             dma(()),
             dma((slots,)),
             dma((peers,)),
@@ -577,7 +600,7 @@
             dma((slots, peers)),
         ],
         compiler_params=pltpu.CompilerParams(
-            collective_id=0, has_side_effects=True, vmem_limit_bytes=56 * 1024 * 1024
+            collective_id=0, has_side_effects=True, vmem_limit_bytes=48 * 1024 * 1024
         ),
         cost_estimate=pl.CostEstimate(flops=flops, bytes_accessed=8 << 20, transcendentals=0),
     )(frame_counts, query_rows, key_rows, value_frames, out_weight, *rope_tables(longest))

time: 52.7 us -> 58.1 us (1.10)
  local copies, waits for them, and re-layouts: 2.65 us -> 9.12 us
  Pallas kernels: 49.9 us -> 48.6 us
    unnamed x1 -> x19, local copies, waits for them, and re-layouts: 2.65 us -> 9.12 us
    pallas_call x1, Pallas kernels: 49.9 us -> 48.6 us  [per_device(): pl.pallas_call(functools.partial(kernel, dims), out_shape=jax.ShapeDtypeS...]
where the time goes in v3:
time: 58.1 us; the launch traced here: 57.7 us
  Pallas kernels  48.6 us (84%)
  local copies, waits for them, and re-layouts  9.12 us (16%)
    pallas_call x1, Pallas kernels, per_device(): pl.pallas_call(functools.partial(kernel, dims), out_shape=jax.ShapeDtypeS...  48.6 us
    unnamed x19, local copies, waits for them, and re-layouts  9.12 us

profile of v3, /device:TPU:0, one launch (start us, length us, event | category | flops | bytes accessed | tf_op | source)
XLA Modules:
  0.0 57.7 jit_solution(7073523682258624564)
XLA Ops:
  0.0 0.0 copy-start
  0.0 1.1 %copy-done = bf16[512,768]{1,0:T(8,128)(2,1)S(1)} copy-done((bf16[512,768]{1,0:T(8,128)(2,1)S(1)}, bf16[512,768]{1,0:T(8,128)(2,1)}, u32[]{:S(2)}) %copy-start) | copy-done | bytes 786456
  1.1 0.0 copy-start.1
  1.1 1.1 %copy-done.1 = bf16[512,768]{1,0:T(8,128)(2,1)S(1)} copy-done((bf16[512,768]{1,0:T(8,128)(2,1)S(1)}, bf16[512,768]{1,0:T(8,128)(2,1)}, u32[]{:S(2)}) %copy-start.1) | copy-done | bytes 786456
  2.3 0.0 copy-start.2
  2.3 1.1 %copy-done.2 = bf16[512,768]{1,0:T(8,128)(2,1)S(1)} copy-done((bf16[512,768]{1,0:T(8,128)(2,1)S(1)}, bf16[512,768]{1,0:T(8,128)(2,1)}, u32[]{:S(2)}) %copy-start.2) | copy-done | bytes 786456
  3.4 0.0 copy-start.3
  3.4 0.9 %copy-done.3 = f32[256,128]{1,0:T(8,128)S(1)} copy-done((f32[256,128]{1,0:T(8,128)S(1)}, f32[256,128]{1,0:T(8,128)}, u32[]{:S(2)}) %copy-start.3) | copy-done | bytes 131096
  4.3 0.0 copy-start.4
  4.3 0.9 %copy-done.4 = f32[256,128]{1,0:T(8,128)S(1)} copy-done((f32[256,128]{1,0:T(8,128)S(1)}, f32[256,128]{1,0:T(8,128)}, u32[]{:S(2)}) %copy-start.4) | copy-done | bytes 131096
  5.2 0.0 copy-start.5
  5.2 0.8 %copy-done.5 = bf16[128,128]{1,0:T(8,128)(2,1)S(1)} copy-done((bf16[128,128]{1,0:T(8,128)(2,1)S(1)}, bf16[128,128]{1,0:T(8,128)(2,1)}, u32[]{:S(2)}) %copy-start.5) | copy-done | bytes 32792
  6.0 0.0 copy-start.6
  6.0 0.7 %copy-done.6 = f32[4,1,128]{2,1,0:T(1,128)S(1)} copy-done((f32[4,1,128]{2,1,0:T(1,128)S(1)}, f32[4,1,128]{2,1,0:T(1,128)}, u32[]{:S(2)}) %copy-start.6) | copy-done | bytes 2072
  6.7 0.0 copy-start.7
  6.7 0.7 %copy-done.7 = f32[4,1,128]{2,1,0:T(1,128)S(1)} copy-done((f32[4,1,128]{2,1,0:T(1,128)S(1)}, f32[4,1,128]{2,1,0:T(1,128)}, u32[]{:S(2)}) %copy-start.7) | copy-done | bytes 2072
  7.3 0.0 copy-start.8
  7.3 0.7 %copy-done.8 = s32[12]{0:T(128)S(1)} copy-done((s32[12]{0:T(128)S(1)}, s32[12]{0:T(128)}, u32[]{:S(2)}) %copy-start.8) | copy-done | bytes 72
  8.0 48.6 %shard_map.100 = bf16[512,1536]{1,0:T(8,128)(2,1)S(1)} custom-call(s32[12]{0:T(128)S(1)} %copy-done.8, bf16[512,768]{1,0:T(8,128)(2,1)S(1)} %copy-done, bf16[512,768]{1,0:T(8,128)(2,1)S(1)} %copy-done.1, bf16[2,256,768]{2,1,0:T(8,128)(2,1)S(1)} %bitcast.1, bf16[768,3072]{1,0:T(8,128)(2,1)} %w_ref.1, f32[256,128]{1,0:T(8,128)S(1)} %copy-done.4, ...), custom_call_target="tpu_custom_call" | custom-call | flops 2415919104 | bytes 8388608 | tf_op jit(solution)/shard_map/pallas_call | solution.py:559
  56.6 1.1 %copy.12 = bf16[512,1536]{1,0:T(8,128)(2,1)} copy(bf16[512,1536]{1,0:T(8,128)(2,1)S(1)} %shard_map.100) | data formatting | bytes 3145728
Async XLA Ops:
  0.0 1.1 %copy-start = (bf16[512,768]{1,0:T(8,128)(2,1)S(1)}, bf16[512,768]{1,0:T(8,128)(2,1)}, u32[]{:S(2)}) copy-start(bf16[512,768]{1,0:T(8,128)(2,1)} %q_ref.1) | copy-start | bytes 2359300
  1.1 1.1 %copy-start.1 = (bf16[512,768]{1,0:T(8,128)(2,1)S(1)}, bf16[512,768]{1,0:T(8,128)(2,1)}, u32[]{:S(2)}) copy-start(bf16[512,768]{1,0:T(8,128)(2,1)} %k_ref.1) | copy-start | bytes 2359300
  2.3 1.1 %copy-start.2 = (bf16[512,768]{1,0:T(8,128)(2,1)S(1)}, bf16[512,768]{1,0:T(8,128)(2,1)}, u32[]{:S(2)}) copy-start(bf16[512,768]{1,0:T(8,128)(2,1)} %param.12) | copy-start | bytes 2359300
  3.4 0.9 %copy-start.3 = (f32[256,128]{1,0:T(8,128)S(1)}, f32[256,128]{1,0:T(8,128)}, u32[]{:S(2)}) copy-start(f32[256,128]{1,0:T(8,128)} %constant.11.clone.sin_hw_ref) | copy-start | bytes 393220
  4.3 0.9 %copy-start.4 = (f32[256,128]{1,0:T(8,128)S(1)}, f32[256,128]{1,0:T(8,128)}, u32[]{:S(2)}) copy-start(f32[256,128]{1,0:T(8,128)} %constant.10.clone.cos_hw_ref) | copy-start | bytes 393220
  5.2 0.8 %copy-start.5 = (bf16[128,128]{1,0:T(8,128)(2,1)S(1)}, bf16[128,128]{1,0:T(8,128)(2,1)}, u32[]{:S(2)}) copy-start(bf16[128,128]{1,0:T(8,128)(2,1)} %constant.14.clone.pairing_ref) | copy-start | bytes 98308
  6.0 0.7 %copy-start.6 = (f32[4,1,128]{2,1,0:T(1,128)S(1)}, f32[4,1,128]{2,1,0:T(1,128)}, u32[]{:S(2)}) copy-start(f32[4,1,128]{2,1,0:T(1,128)} %constant.13.clone.sin_t_ref) | copy-start | bytes 6148
  6.7 0.7 %copy-start.7 = (f32[4,1,128]{2,1,0:T(1,128)S(1)}, f32[4,1,128]{2,1,0:T(1,128)}, u32[]{:S(2)}) copy-start(f32[4,1,128]{2,1,0:T(1,128)} %constant.12.clone.cos_t_ref) | copy-start | bytes 6148
  7.3 0.7 %copy-start.8 = (s32[12]{0:T(128)S(1)}, s32[12]{0:T(128)}, u32[]{:S(2)}) copy-start(s32[12]{0:T(128)} %counts_ref.1) | copy-start | bytes 148

commit v4 on v3

--- a/solution.py
+++ b/solution.py
@@ -338,9 +338,10 @@
             for f in range(own_frames):
                 k_own[head, f] = rotated(k_in, f, head)
         send(k_copy, slot)
-        if slot == 0:
-            loads[-1].wait()
-        for head in slot_heads:
+
+    loads[-1].wait()
+    for slot in range(slots):
+        for head in range(slot * group, slot * group + sized(slot)):
             for f in range(own_frames):
                 part = slice(f * FRAME, (f + 1) * FRAME)
                 q_own[head, part, :] = rotated(q_in, f, head)
@@ -381,8 +382,6 @@
         start_halos(slot, 0)
 
     def settle(slot):
-        for d in range(1, group):
-            q_copy(slot, d, from_member(d), member).wait_recv()
         for what in (1, 0):
             for d in range(1, reach + 1):
                 for up in (True, False):
@@ -393,9 +392,13 @@
 
     ones = jnp.ones((FRAME, HEAD_DIM), jnp.bfloat16)
 
-    def attend(slot, step, carry):
-        d = lax.rem(step + 1, group)
-        target = to_member(d)
+    def attend(slot, d, carry):
+        target = from_member(d)
+
+        @pl.when(d > 0)
+        def _():
+            q_copy(slot, d, target, member).wait_recv()
+
         for f in range(own_frames):
             place = target * own_frames + f
             start, stop = clip_span(counts_ref, clips, longest, first_frame + place)
@@ -436,38 +439,34 @@
 
         @pl.when(d > 0)
         def _():
-            o_copy(slot, d, member, target).start()
+            o_copy(slot, group - d, member, target).start()
 
         return carry
 
-    @pl.when(have[0])
-    def _():
-        spread(0)
-        settle(0)
-        lax.fori_loop(0, group // 2, functools.partial(attend, 0), 0)
-
-    own_weight.start()
-    for d in range(1, peers):
-        w_copy(d).start()
-
-    for slot in range(1, slots + 1):
-        if slot < slots:
-
-            @pl.when(have[slot])
-            def _():
-                spread(slot)
-
-        @pl.when(have[slot - 1])
-        def _():
-            lax.fori_loop(group // 2, group, functools.partial(attend, slot - 1), 0)
-            o_all[tp, head_of(member, slot - 1)] = o_mine[slot - 1, query_rows(member), :]
-
-        if slot < slots:
-
-            @pl.when(have[slot])
-            def _():
-                settle(slot)
-                lax.fori_loop(0, group // 2, functools.partial(attend, slot), 0)
+    for slot in range(slots):
+
+        @pl.when(have[slot])
+        def _():
+            spread(slot)
+
+    for slot in range(slots):
+
+        @pl.when(have[slot])
+        def _():
+            settle(slot)
+            lax.fori_loop(0, 1, functools.partial(attend, slot), 0)
+            o_all[tp, head_of(member, slot)] = o_mine[slot, query_rows(member), :]
+
+        if slot == 0:
+            own_weight.start()
+            for d in range(1, peers):
+                w_copy(d).start()
+
+    for slot in range(slots):
+
+        @pl.when(have[slot])
+        def _():
+            lax.fori_loop(1, group, functools.partial(attend, slot), 0)
 
     chunk = 256
 
@@ -562,7 +561,7 @@
         in_specs=[
             pl.BlockSpec(memory_space=pltpu.SMEM),
         ]
-        + [pl.BlockSpec(memory_space=pltpu.HBM)] * 9,
+        + [pl.BlockSpec(memory_space=pl.ANY)] * 9,
         out_specs=vmem,
         scratch_shapes=[
             pltpu.VMEM((rows, features), bf16),
@@ -600,7 +599,7 @@
             dma((slots, peers)),
         ],
         compiler_params=pltpu.CompilerParams(
-            collective_id=0, has_side_effects=True, vmem_limit_bytes=48 * 1024 * 1024
+            collective_id=0, has_side_effects=True, vmem_limit_bytes=56 * 1024 * 1024
         ),
         cost_estimate=pl.CostEstimate(flops=flops, bytes_accessed=8 << 20, transcendentals=0),
     )(frame_counts, query_rows, key_rows, value_frames, out_weight, *rope_tables(longest))

time: 58.1 us -> 52.5 us (0.904); the launches traced: 57.7 us -> 51.5 us
  local copies, waits for them, and re-layouts: 9.12 us -> 2.65 us
    unnamed x19 -> x1, local copies, waits for them, and re-layouts: 9.12 us -> 2.65 us
where the time goes in v4:
time: 52.5 us; the launch traced here: 51.5 us
  Pallas kernels  48.8 us (93%)
  local copies, waits for them, and re-layouts  2.65 us (5%)
    pallas_call x1, Pallas kernels, per_device(): pl.pallas_call(functools.partial(kernel, dims), out_shape=jax.ShapeDtypeS...  48.8 us
    unnamed x1, local copies, waits for them, and re-layouts  2.65 us

profile of v4, /device:TPU:0, one launch (start us, length us, event | category | flops | bytes accessed | tf_op | source)
XLA Modules:
  0.0 51.5 jit_solution(902868254314744652)
XLA Ops:
  0.0 48.8 %shard_map.100 = bf16[512,1536]{1,0:T(8,128)(2,1)} custom-call(s32[12]{0:T(128)} %counts_ref.1, bf16[512,768]{1,0:T(8,128)(2,1)} %q_ref.1, bf16[512,768]{1,0:T(8,128)(2,1)} %k_ref.1, bf16[2,256,768]{2,1,0:T(8,128)(2,1)} %bitcast.1, bf16[768,3072]{1,0:T(8,128)(2,1)} %w_ref.1, f32[256,128]{1,0:T(8,128)} %constant.10.clone.cos_hw_ref, ...), custom_call_target="tpu_custom_call" | custom-call | flops 2415919104 | bytes 8388608 | tf_op jit(solution)/shard_map/pallas_call | solution.py:558
  48.8 2.7 %copy.12 = bf16[512,1536]{1,0:T(8,128)(2,1)} copy(bf16[512,1536]{1,0:T(8,128)(2,1)} %shard_map.100) | data formatting | bytes 3145728

commit v5 on v4

--- a/solution.py
+++ b/solution.py
@@ -82,6 +82,7 @@
     q_all,
     k_all,
     v_all,
+    v_turned,
     o_mine,
     o_all,
     w_all,
@@ -390,7 +391,13 @@
                     def _():
                         halo_copy(slot, what, d, up, True).wait_recv()
 
-    ones = jnp.ones((FRAME, HEAD_DIM), jnp.bfloat16)
+    def turn(slot):
+        def body(frame, carry):
+            v_turned[slot][frame, :HEAD_DIM, :] = v_all[slot][frame].T
+            v_turned[slot][frame, HEAD_DIM:, :] = jnp.ones((16, FRAME), jnp.bfloat16)
+            return carry
+
+        lax.fori_loop(0, span + 2 * halo, body, 0)
 
     def attend(slot, d, carry):
         target = from_member(d)
@@ -409,33 +416,32 @@
             largest = None
             for i in range(longest):
                 part = lax.dot_general(
+                    k_all[slot][first_key + i],
                     queries,
-                    k_all[slot][first_key + i],
                     (((1,), (1,)), ((), ())),
                     preferred_element_type=jnp.float32,
                 )
-                top = jnp.max(part, axis=1, keepdims=True)
-                same = jnp.full((FRAME, 1), start + i, jnp.int32) < stop
+                top = jnp.max(part, axis=0, keepdims=True)
+                same = jnp.full((1, FRAME), start + i, jnp.int32) < stop
                 kept = jnp.where(same, top, NEG_FILL)
                 largest = kept if i == 0 else jnp.maximum(largest, kept)
-                both = jnp.concatenate([v_all[slot][first_key + i], ones], axis=1)
-                in_clip = jnp.full(both.shape, start + i, jnp.int32) < stop
+                turned = v_turned[slot][first_key + i]
+                in_clip = jnp.full(turned.shape, start + i, jnp.int32) < stop
                 scores.append(part)
                 tops.append(top)
                 inside.append(same)
-                values.append(jnp.where(in_clip, both, jnp.zeros_like(both)))
+                values.append(jnp.where(in_clip, turned, jnp.zeros_like(turned)))
             weights = [
                 jnp.exp2((part - jnp.where(same, largest, top)) * scale).astype(jnp.bfloat16)
                 for part, same, top in zip(scores, inside, tops)
             ]
             summed = jnp.dot(
-                jnp.concatenate(weights, axis=1),
-                jnp.concatenate(values, axis=0),
+                jnp.concatenate(values, axis=1),
+                jnp.concatenate(weights, axis=0),
                 preferred_element_type=jnp.float32,
             )
-            o_mine[slot, here, :] = (
-                summed[:, :HEAD_DIM] / summed[:, HEAD_DIM:]
-            ).astype(jnp.bfloat16)
+            attended = summed[:HEAD_DIM] / summed[HEAD_DIM : HEAD_DIM + 1]
+            o_mine[slot, here, :] = attended.T.astype(jnp.bfloat16)
 
         @pl.when(d > 0)
         def _():
@@ -454,6 +460,7 @@
         @pl.when(have[slot])
         def _():
             settle(slot)
+            turn(slot)
             lax.fori_loop(0, 1, functools.partial(attend, slot), 0)
             o_all[tp, head_of(member, slot)] = o_mine[slot, query_rows(member), :]
 
@@ -576,6 +583,7 @@
             pltpu.VMEM((slots, group * rows, HEAD_DIM), bf16),
             [pltpu.VMEM((span + 2 * halo, FRAME, HEAD_DIM), bf16)] * slots,
             [pltpu.VMEM((span + 2 * halo, FRAME, HEAD_DIM), bf16)] * slots,
+            [pltpu.VMEM((span + 2 * halo, HEAD_DIM + 16, FRAME), bf16)] * slots,
             pltpu.VMEM((slots, group * rows, HEAD_DIM), bf16),
             pltpu.VMEM((peers, heads, rows, HEAD_DIM), bf16),
             pltpu.VMEM((peers, features, columns), bf16),

time: 52.5 us -> 54.2 us (1.032)
  Pallas kernels: 48.8 us -> 50.5 us
    pallas_call x1, Pallas kernels: 48.8 us -> 50.5 us  [per_device(): pl.pallas_call(functools.partial(kernel, dims), out_shape=jax.ShapeDtypeS...]
where the time goes in v5:
time: 54.2 us; the launch traced here: 53.2 us
  Pallas kernels  50.5 us (93%)
  local copies, waits for them, and re-layouts  2.65 us (5%)
    pallas_call x1, Pallas kernels, per_device(): pl.pallas_call(functools.partial(kernel, dims), out_shape=jax.ShapeDtypeS...  50.5 us
    unnamed x1, local copies, waits for them, and re-layouts  2.65 us

profile of v5, /device:TPU:0, one launch (start us, length us, event | category | flops | bytes accessed | tf_op | source)
XLA Modules:
  0.0 53.2 jit_solution(17594848136032808660)
XLA Ops:
  0.0 50.5 %shard_map.100 = bf16[512,1536]{1,0:T(8,128)(2,1)} custom-call(s32[12]{0:T(128)} %counts_ref.1, bf16[512,768]{1,0:T(8,128)(2,1)} %q_ref.1, bf16[512,768]{1,0:T(8,128)(2,1)} %k_ref.1, bf16[2,256,768]{2,1,0:T(8,128)(2,1)} %bitcast.1, bf16[768,3072]{1,0:T(8,128)(2,1)} %w_ref.1, f32[256,128]{1,0:T(8,128)} %constant.10.clone.cos_hw_ref, ...), custom_call_target="tpu_custom_call" | custom-call | flops 2415919104 | bytes 8388608 | tf_op jit(solution)/shard_map/pallas_call | solution.py:565
  50.6 2.7 %copy.12 = bf16[512,1536]{1,0:T(8,128)(2,1)} copy(bf16[512,1536]{1,0:T(8,128)(2,1)} %shard_map.100) | data formatting | bytes 3145728

commit v6 on v3

--- a/solution.py
+++ b/solution.py
@@ -322,29 +322,38 @@
         w_local,
     )
 
-    for slot in range(slots):
-        slot_heads = range(slot * group, slot * group + sized(slot))
+    def give_values(slot):
         send(v_copy, slot)
 
         @pl.when(have[slot])
         def _():
             v_stay(slot).start()
 
-        if slot == 0:
-            for load in loads[:-1]:
-                load.wait()
-            angles()
-        for head in slot_heads:
+    def give_keys(slot):
+        for head in range(slot * group, slot * group + sized(slot)):
             for f in range(own_frames):
                 k_own[head, f] = rotated(k_in, f, head)
         send(k_copy, slot)
-        if slot == 0:
-            loads[-1].wait()
-        for head in slot_heads:
+
+    def give_queries(slot):
+        for head in range(slot * group, slot * group + sized(slot)):
             for f in range(own_frames):
                 part = slice(f * FRAME, (f + 1) * FRAME)
                 q_own[head, part, :] = rotated(q_in, f, head)
         send(q_copy, slot)
+
+    give_values(0)
+    for load in loads[:-1]:
+        load.wait()
+    angles()
+    give_keys(0)
+    loads[-1].wait()
+    for slot in range(slots):
+        if slot + 1 < slots:
+            give_values(slot + 1)
+        give_queries(slot)
+        if slot + 1 < slots:
+            give_keys(slot + 1)
 
     scale = HEAD_DIM**-0.5 * math.log2(math.e)
 
@@ -381,8 +390,6 @@
         start_halos(slot, 0)
 
     def settle(slot):
-        for d in range(1, group):
-            q_copy(slot, d, from_member(d), member).wait_recv()
         for what in (1, 0):
             for d in range(1, reach + 1):
                 for up in (True, False):
@@ -391,60 +398,54 @@
                     def _():
                         halo_copy(slot, what, d, up, True).wait_recv()
 
-    ones = jnp.ones((FRAME, HEAD_DIM), jnp.bfloat16)
-
-    def attend(slot, step, carry):
-        d = lax.rem(step + 1, group)
-        target = to_member(d)
+    column = lax.broadcasted_iota(jnp.int32, (1, longest * FRAME), 1)
+
+    def attend(slot, d, carry):
+        target = from_member(d)
+
+        @pl.when(d > 0)
+        def _():
+            q_copy(slot, d, target, member).wait_recv()
+
         for f in range(own_frames):
             place = target * own_frames + f
             start, stop = clip_span(counts_ref, clips, longest, first_frame + place)
             here = pl.ds(pl.multiple_of(place * FRAME, FRAME), FRAME)
             first_key = start - first_frame + halo
             queries = q_all[slot, here, :]
-            scores, tops, values, inside = [], [], [], []
-            largest = None
-            for i in range(longest):
-                part = lax.dot_general(
-                    queries,
-                    k_all[slot][first_key + i],
-                    (((1,), (1,)), ((), ())),
-                    preferred_element_type=jnp.float32,
-                )
-                top = jnp.max(part, axis=1, keepdims=True)
-                same = jnp.full((FRAME, 1), start + i, jnp.int32) < stop
-                kept = jnp.where(same, top, NEG_FILL)
-                largest = kept if i == 0 else jnp.maximum(largest, kept)
-                both = jnp.concatenate([v_all[slot][first_key + i], ones], axis=1)
-                in_clip = jnp.full(both.shape, start + i, jnp.int32) < stop
-                scores.append(part)
-                tops.append(top)
-                inside.append(same)
-                values.append(jnp.where(in_clip, both, jnp.zeros_like(both)))
-            weights = [
-                jnp.exp2((part - jnp.where(same, largest, top)) * scale).astype(jnp.bfloat16)
-                for part, same, top in zip(scores, inside, tops)
-            ]
+            keys = jnp.concatenate(
+                [k_all[slot][first_key + i] for i in range(longest)], axis=0
+            )
+            values = jnp.concatenate(
+                [v_all[slot][first_key + i] for i in range(longest)], axis=0
+            )
+            scores = lax.dot_general(
+                queries, keys, (((1,), (1,)), ((), ())), preferred_element_type=jnp.float32
+            )
+            scores = jnp.where(column < (stop - start) * FRAME, scores, NEG_FILL)
+            largest = jnp.max(scores, axis=1, keepdims=True)
+            expo = jnp.exp2((scores - largest) * scale)
+            total = jnp.sum(expo, axis=1, keepdims=True)
             summed = jnp.dot(
-                jnp.concatenate(weights, axis=1),
-                jnp.concatenate(values, axis=0),
-                preferred_element_type=jnp.float32,
+                expo.astype(jnp.bfloat16), values, preferred_element_type=jnp.float32
             )
-            o_mine[slot, here, :] = (
-                summed[:, :HEAD_DIM] / summed[:, HEAD_DIM:]
-            ).astype(jnp.bfloat16)
+            o_mine[slot, here, :] = (summed / total).astype(jnp.bfloat16)
 
         @pl.when(d > 0)
         def _():
-            o_copy(slot, d, member, target).start()
+            o_copy(slot, group - d, member, target).start()
 
         return carry
+
+    def attend_some(slot, low, high):
+        lax.fori_loop(low, high, functools.partial(attend, slot), 0)
 
     @pl.when(have[0])
     def _():
         spread(0)
         settle(0)
-        lax.fori_loop(0, group // 2, functools.partial(attend, 0), 0)
+        attend_some(0, 0, 2)
+        o_all[tp, head_of(member, 0)] = o_mine[0, query_rows(member), :]
 
     own_weight.start()
     for d in range(1, peers):
@@ -459,15 +460,15 @@
 
         @pl.when(have[slot - 1])
         def _():
-            lax.fori_loop(group // 2, group, functools.partial(attend, slot - 1), 0)
-            o_all[tp, head_of(member, slot - 1)] = o_mine[slot - 1, query_rows(member), :]
+            attend_some(slot - 1, 2, group)
 
         if slot < slots:
 
             @pl.when(have[slot])
             def _():
                 settle(slot)
-                lax.fori_loop(0, group // 2, functools.partial(attend, slot), 0)
+                attend_some(slot, 0, 2)
+                o_all[tp, head_of(member, slot)] = o_mine[slot, query_rows(member), :]
 
     chunk = 256
 
@@ -562,7 +563,7 @@
         in_specs=[
             pl.BlockSpec(memory_space=pltpu.SMEM),
         ]
-        + [pl.BlockSpec(memory_space=pltpu.HBM)] * 9,
+        + [pl.BlockSpec(memory_space=pl.ANY)] * 9,
         out_specs=vmem,
         scratch_shapes=[
             pltpu.VMEM((rows, features), bf16),
@@ -600,7 +601,7 @@
             dma((slots, peers)),
         ],
         compiler_params=pltpu.CompilerParams(
-            collective_id=0, has_side_effects=True, vmem_limit_bytes=48 * 1024 * 1024
+            collective_id=0, has_side_effects=True, vmem_limit_bytes=56 * 1024 * 1024
         ),
         cost_estimate=pl.CostEstimate(flops=flops, bytes_accessed=8 << 20, transcendentals=0),
     )(frame_counts, query_rows, key_rows, value_frames, out_weight, *rope_tables(longest))

time: 58.1 us -> 52.2 us (0.90)
  local copies, waits for them, and re-layouts: 9.12 us -> 2.65 us
    unnamed x19 -> x1, local copies, waits for them, and re-layouts: 9.12 us -> 2.65 us
where the time goes in v6:
time: 52.2 us; the launch traced here: 51.6 us
  Pallas kernels  48.9 us (94%)
  local copies, waits for them, and re-layouts  2.65 us (5%)
    pallas_call x1, Pallas kernels, per_device(): pl.pallas_call(functools.partial(kernel, dims), out_shape=jax.ShapeDtypeS...  48.9 us
    unnamed x1, local copies, waits for them, and re-layouts  2.65 us

profile of v6, /device:TPU:0, one launch (start us, length us, event | category | flops | bytes accessed | tf_op | source)
XLA Modules:
  0.0 51.6 jit_solution(6334570671423053720)
XLA Ops:
  0.0 48.9 %shard_map.100 = bf16[512,1536]{1,0:T(8,128)(2,1)} custom-call(s32[12]{0:T(128)} %counts_ref.1, bf16[512,768]{1,0:T(8,128)(2,1)} %q_ref.1, bf16[512,768]{1,0:T(8,128)(2,1)} %k_ref.1, bf16[2,256,768]{2,1,0:T(8,128)(2,1)} %bitcast.1, bf16[768,3072]{1,0:T(8,128)(2,1)} %w_ref.1, f32[256,128]{1,0:T(8,128)} %constant.10.clone.cos_hw_ref, ...), custom_call_target="tpu_custom_call" | custom-call | flops 2415919104 | bytes 8388608 | tf_op jit(solution)/shard_map/pallas_call | solution.py:560
  48.9 2.7 %copy.12 = bf16[512,1536]{1,0:T(8,128)(2,1)} copy(bf16[512,1536]{1,0:T(8,128)(2,1)} %shard_map.100) | data formatting | bytes 3145728

commit v7 on v6

--- a/solution.py
+++ b/solution.py
@@ -538,6 +538,20 @@
                         halo_copy(slot, what, d, up, False).wait_send()
 
 
+def hand_over(pieces, from_ref, to_ref, done):
+    rows = from_ref.shape[0] // pieces
+    copies = [
+        pltpu.make_async_copy(
+            from_ref.at[pl.ds(i * rows, rows)], to_ref.at[pl.ds(i * rows, rows)], done.at[i]
+        )
+        for i in range(pieces)
+    ]
+    for copy in copies:
+        copy.start()
+    for copy in copies:
+        copy.wait()
+
+
 def per_device(seq, peers, query_rows, key_rows, value_rows, frame_counts, out_weight):
     rows, features = query_rows.shape
     heads = features // HEAD_DIM
@@ -557,7 +571,7 @@
     dma = pltpu.SemaphoreType.DMA
     bf16 = jnp.bfloat16
     flops = 2 * rows * features * out_weight.shape[1]
-    return pl.pallas_call(
+    mixed = pl.pallas_call(
         functools.partial(kernel, dims),
         out_shape=jax.ShapeDtypeStruct((rows, columns), bf16),
         in_specs=[
@@ -605,6 +619,16 @@
         ),
         cost_estimate=pl.CostEstimate(flops=flops, bytes_accessed=8 << 20, transcendentals=0),
     )(frame_counts, query_rows, key_rows, value_frames, out_weight, *rope_tables(longest))
+    pieces = 8
+    return pl.pallas_call(
+        functools.partial(hand_over, pieces),
+        out_shape=jax.ShapeDtypeStruct((rows, columns), bf16),
+        in_specs=[pl.BlockSpec(memory_space=pl.ANY)],
+        out_specs=pl.BlockSpec(memory_space=pl.ANY),
+        scratch_shapes=[dma((pieces,))],
+        compiler_params=pltpu.CompilerParams(vmem_limit_bytes=56 * 1024 * 1024),
+        cost_estimate=pl.CostEstimate(flops=0, bytes_accessed=4 << 20, transcendentals=0),
+    )(mixed)
 
 
 def solution(mesh):

time: 52.2 us -> 98.4 us (1.89)
  Pallas kernels: 48.9 us -> 97.8 us
  local copies, waits for them, and re-layouts: 2.65 us -> 0 us
    pallas_call x0 -> x1, Pallas kernels: none -> 48.8 us  [per_device(): pl.pallas_call(functools.partial(hand_over, pieces), out_shape=jax.ShapeD...]
    unnamed x1 -> x0, local copies, waits for them, and re-layouts: 2.65 us -> none
where the time goes in v7:
time: 98.4 us; the launch traced here: 97.8 us
  Pallas kernels  97.8 us (99%)
    pallas_call x1, Pallas kernels, per_device(): pl.pallas_call(functools.partial(kernel, dims), out_shape=jax.ShapeDtypeS...  48.9 us
    pallas_call x1, Pallas kernels, per_device(): pl.pallas_call(functools.partial(hand_over, pieces), out_shape=jax.ShapeD...  48.8 us

profile of v7, /device:TPU:0, one launch (start us, length us, event | category | flops | bytes accessed | tf_op | source)
XLA Modules:
  0.0 97.8 jit_solution(6622563927364219863)
XLA Ops:
  0.0 48.9 %shard_map.100.from_ref = bf16[512,1536]{1,0:T(8,128)(2,1)} custom-call(s32[12]{0:T(128)} %counts_ref.1, bf16[512,768]{1,0:T(8,128)(2,1)} %q_ref.1, bf16[512,768]{1,0:T(8,128)(2,1)} %k_ref.1, bf16[2,256,768]{2,1,0:T(8,128)(2,1)} %bitcast.1, bf16[768,3072]{1,0:T(8,128)(2,1)} %w_ref.1, f32[256,128]{1,0:T(8,128)} %constant.10.clone.cos_hw_ref, ...), custom_call_target="tpu_custom_call" | custom-call | flops 2415919104 | bytes 8388608 | tf_op jit(solution)/shard_map/pallas_call | solution.py:574
  48.9 48.8 %shard_map.101 = bf16[512,1536]{1,0:T(8,128)(2,1)} custom-call(bf16[512,1536]{1,0:T(8,128)(2,1)} %shard_map.100.from_ref), custom_call_target="tpu_custom_call" | custom-call | bytes 4194304 | tf_op jit(solution)/shard_map/pallas_call | solution.py:623

commit v8 on v6

--- a/solution.py
+++ b/solution.py
@@ -538,6 +538,10 @@
                         halo_copy(slot, what, d, up, False).wait_send()
 
 
+def hand_over(from_ref, to_ref):
+    to_ref[...] = from_ref[...]
+
+
 def per_device(seq, peers, query_rows, key_rows, value_rows, frame_counts, out_weight):
     rows, features = query_rows.shape
     heads = features // HEAD_DIM
@@ -557,7 +561,7 @@
     dma = pltpu.SemaphoreType.DMA
     bf16 = jnp.bfloat16
     flops = 2 * rows * features * out_weight.shape[1]
-    return pl.pallas_call(
+    mixed = pl.pallas_call(
         functools.partial(kernel, dims),
         out_shape=jax.ShapeDtypeStruct((rows, columns), bf16),
         in_specs=[
@@ -605,6 +609,15 @@
         ),
         cost_estimate=pl.CostEstimate(flops=flops, bytes_accessed=8 << 20, transcendentals=0),
     )(frame_counts, query_rows, key_rows, value_frames, out_weight, *rope_tables(longest))
+    block = pl.BlockSpec((rows // 4, columns), lambda i: (i, 0))
+    return pl.pallas_call(
+        hand_over,
+        grid=(4,),
+        out_shape=jax.ShapeDtypeStruct((rows, columns), bf16),
+        in_specs=[block],
+        out_specs=block,
+        compiler_params=pltpu.CompilerParams(vmem_limit_bytes=56 * 1024 * 1024),
+    )(mixed)
 
 
 def solution(mesh):

time: 52.2 us -> 53.1 us (1.017)
  Pallas kernels: 48.9 us -> 52.5 us
  local copies, waits for them, and re-layouts: 2.65 us -> 0 us
    pallas_call x0 -> x1, Pallas kernels: none -> 3.57 us  [per_device(): pl.pallas_call(hand_over, grid=(4,), out_shape=jax.ShapeDtypeStruct((rows...]
    unnamed x1 -> x0, local copies, waits for them, and re-layouts: 2.65 us -> none
where the time goes in v8:
time: 53.1 us; the launch traced here: 52.5 us
  Pallas kernels  52.5 us (99%)
    pallas_call x1, Pallas kernels, per_device(): pl.pallas_call(functools.partial(kernel, dims), out_shape=jax.ShapeDtypeS...  48.9 us
    pallas_call x1, Pallas kernels, per_device(): pl.pallas_call(hand_over, grid=(4,), out_shape=jax.ShapeDtypeStruct((rows...  3.57 us

profile of v8, /device:TPU:0, one launch (start us, length us, event | category | flops | bytes accessed | tf_op | source)
XLA Modules:
  0.0 52.5 jit_solution(15745364446224169547)
XLA Ops:
  0.0 48.9 %shard_map.100.from_ref = bf16[512,1536]{1,0:T(8,128)(2,1)} custom-call(s32[12]{0:T(128)} %counts_ref.1, bf16[512,768]{1,0:T(8,128)(2,1)} %q_ref.1, bf16[512,768]{1,0:T(8,128)(2,1)} %k_ref.1, bf16[2,256,768]{2,1,0:T(8,128)(2,1)} %bitcast.1, bf16[768,3072]{1,0:T(8,128)(2,1)} %w_ref.1, f32[256,128]{1,0:T(8,128)} %constant.10.clone.cos_hw_ref, ...), custom_call_target="tpu_custom_call" | custom-call | flops 2415919104 | bytes 8388608 | tf_op jit(solution)/shard_map/pallas_call | solution.py:564
  48.9 3.6 %shard_map.101 = bf16[512,1536]{1,0:T(8,128)(2,1)} custom-call(bf16[512,1536]{1,0:T(8,128)(2,1)} %shard_map.100.from_ref), custom_call_target="tpu_custom_call" | custom-call | tf_op jit(solution)/shard_map/pallas_call | solution.py:613
